TPU v7x, 256 devices: a whole 4x4x8 slice. The times are simulated.
256 devices in a mesh: wide: 64 (over y, z, core), narrow: 4 (over x).
Axes of the slice: x: 4, y: 4, z: 8, core: 2. Of those that a mesh axis runs over, the one named last changes fastest.
Arguments:
- item_owner: int32 [512, 512, 1], P(('wide', 'narrow')), may hold values from 0 to 63; in each aligned block of 1024 rows (0 to 1023, 1024 to 2047, ..., all dimensions but the last counted through in order) at most 24 rows name the same one
- item_row: int32 [512, 512], P(('wide', 'narrow')), may hold values from 0 to 1023
- hot_row: int32 [512, 512], P(('wide', 'narrow')), may hold values from 0 to 1023
- hot_flag: int32 [512, 512], P(('wide', 'narrow')), may hold values from 0 to 1, as said below
- seq_length: int32 [512], P(('wide', 'narrow')), may hold values from 256 to 512, as said below
- cold_table: bfloat16 [65536, 512], P('wide'), may hold values from -6 to 6
- hot_table: bfloat16 [1024, 512], replicated, may hold values from -6 to 6
- proj_weight: bfloat16 [512, 2048], replicated, may hold values from -0.25 to 0.25
- out_weight: bfloat16 [512, 512], replicated, may hold values from -0.25 to 0.25
- norm_gain: float32 [1, 512], replicated, may hold values from 0.5 to 1.5
- cotangent: bfloat16 [512, 512, 512], P(('wide', 'narrow')), may hold values from -6 to 6
Outputs:
- proj_grad: float32 [512, 2048], P(None, 'wide')
- out_grad: float32 [512, 512], P(None, 'wide')
- gain_grad: float32 [1, 512], P(None, 'wide')
- cold_grad: float32 [65536, 512], P(('wide', 'narrow'))
- hot_grad: float32 [1024, 512], P(('wide', 'narrow'))
Inputs may be any that keep to these rules, and one draw needn't show every extreme that they name: `item_owner`: at most 24 of the token slots of one device (padding and hot ones included) name one owner; in every draw some device's slots name some owner exactly 24 times. `seq_length`: each is a multiple of 128; some history has the full 512. `hot_flag`: in every draw all token slots of some device are hot; that device's slots name 1024 different hot rows.
All inputs are finite; a program needn't handle non-finite values.
Results may differ from a plain program's by a relative error of at most 0.014.
Values may be sent and summed in bfloat16 or wider, within the bound.
A program may use at most 128 MiB of HBM per device.

v0:
```python
import jax
import jax.numpy as jnp
from jax import lax
from jax.sharding import PartitionSpec as P

HEADS = 4


epsilon = 1e-05


def layer_norm(values):
    center = values - jnp.mean(values, axis=-1, keepdims=True)
    spread = jnp.mean(center * center, axis=-1, keepdims=True)
    return center * lax.rsqrt(spread + epsilon)


def layer_grads(embedded, cotan, length, proj_weight, out_weight, norm_gain):
    seq_len, width = embedded.shape
    head_width = width // HEADS
    positions = jnp.arange(seq_len, dtype=jnp.int32)
    live = (positions < length).astype(jnp.float32)[:, None]
    masked = (cotan.astype(jnp.float32) * live).astype(jnp.bfloat16)

    def normalize(rows, scale):
        return layer_norm(rows) * scale

    normed_full, norm_back = jax.vjp(normalize, embedded.astype(jnp.float32), norm_gain)
    normed = normed_full.astype(jnp.bfloat16)
    projected = jnp.dot(normed, proj_weight, preferred_element_type=jnp.float32)
    allowed = ((positions[None, :] <= positions[:, None]) & (positions[None, :] < length)).astype(
        jnp.float32
    )
    inverse = 1.0 / length.astype(jnp.float32)

    def mixing(proj_rows):
        acted = jax.nn.silu(proj_rows).astype(jnp.bfloat16)
        gate_part = acted[:, :width].astype(jnp.float32)
        value_part = (
            acted[:, width : 2 * width].astype(jnp.float32).reshape(seq_len, HEADS, head_width)
        )
        query_part = (
            acted[:, 2 * width : 3 * width].astype(jnp.float32).reshape(seq_len, HEADS, head_width)
        )
        key_part = acted[:, 3 * width :].astype(jnp.float32).reshape(seq_len, HEADS, head_width)
        scores = jnp.einsum("qhd,khd->hqk", query_part, key_part) * head_width ** (-0.5)
        weights = (jax.nn.silu(scores) * allowed[None] * inverse).astype(jnp.bfloat16)
        per_head = jnp.einsum("hqk,khd->qhd", weights.astype(jnp.float32), value_part).reshape(
            seq_len, width
        )
        return (layer_norm(per_head) * gate_part).astype(jnp.bfloat16)

    mixed, mix_back = jax.vjp(mixing, projected)
    out_part = jnp.dot(mixed.T, masked, preferred_element_type=jnp.float32)
    mixed_cot = jnp.dot(masked, out_weight.T, preferred_element_type=jnp.float32).astype(
        jnp.bfloat16
    )
    proj_cot = mix_back(mixed_cot)[0].astype(jnp.bfloat16)
    proj_part = jnp.dot(normed.T, proj_cot, preferred_element_type=jnp.float32)
    normed_cot = jnp.dot(proj_cot, proj_weight.T, preferred_element_type=jnp.float32)
    emb_cot, gain_part = norm_back(normed_cot)
    emb_grad = ((masked.astype(jnp.float32) + emb_cot) * live).astype(jnp.bfloat16)
    return (emb_grad, proj_part, out_part, gain_part)


def local(
    item_owner,
    item_row,
    hot_row,
    hot_flag,
    seq_length,
    cold_table,
    hot_table,
    proj_weight,
    out_weight,
    norm_gain,
    cotangent,
):
    sequences, seq_len = item_row.shape
    width = cold_table.shape[1]
    shard_rows = cold_table.shape[0]
    tokens = sequences * seq_len
    owners = lax.axis_size("wide")
    capacity = max(2, (3 * tokens + 2 * owners - 1) // (2 * owners))
    owner_flat = item_owner.reshape(tokens)
    row_flat = item_row.reshape(tokens)
    hot_flat = hot_row.reshape(tokens)
    is_hot = (hot_flag.reshape(tokens) == 1)[:, None]
    onehot = (owner_flat[:, None] == jnp.arange(owners, dtype=jnp.int32)[None, :]).astype(jnp.int32)
    within = jnp.sum(jnp.cumsum(onehot, axis=0) * onehot, axis=1) - 1
    slot_index = owner_flat * capacity + within
    request = (
        jnp.zeros((owners * capacity,), jnp.int32)
        .at[slot_index]
        .set(row_flat)
        .reshape(owners, capacity)
    )
    wanted = lax.all_to_all(request, "wide", split_axis=0, concat_axis=0, tiled=True)
    found = cold_table[wanted]
    replies = lax.all_to_all(found, "wide", split_axis=0, concat_axis=0, tiled=True)
    from_cold = replies.reshape(owners * capacity, width)[slot_index]
    from_hot = hot_table[hot_flat]
    embedded = jnp.where(is_hot, from_hot, from_cold).reshape(sequences, seq_len, width)

    def step(carry, inputs):
        rows, cotan, length = inputs
        emb_grad, proj_part, out_part, gain_part = layer_grads(
            rows, cotan, length, proj_weight, out_weight, norm_gain
        )
        return ((carry[0] + proj_part, carry[1] + out_part, carry[2] + gain_part), emb_grad)

    start = (
        jnp.zeros((width, 4 * width), jnp.float32),
        jnp.zeros((width, width), jnp.float32),
        jnp.zeros((1, width), jnp.float32),
    )
    totals, emb_grads = lax.scan(step, start, (embedded, cotangent, seq_length))
    flat_grad = emb_grads.reshape(tokens, width)
    cold_terms = jnp.where(is_hot, jnp.zeros_like(flat_grad), flat_grad)
    cold_send = (
        jnp.zeros((owners * capacity, width), jnp.bfloat16)
        .at[slot_index]
        .set(cold_terms)
        .reshape(owners, capacity, width)
    )
    arrived = lax.all_to_all(cold_send, "wide", split_axis=0, concat_axis=0, tiled=True)
    row_sums = (
        jnp.zeros((shard_rows, width), jnp.float32)
        .at[wanted.reshape(-1)]
        .add(arrived.reshape(-1, width).astype(jnp.float32))
    )
    cold_grad = lax.psum_scatter(row_sums, "narrow", scatter_dimension=0, tiled=True)
    hot_terms = jnp.where(is_hot, flat_grad.astype(jnp.float32), 0.0)
    hot_sums = jnp.zeros((hot_table.shape[0], width), jnp.float32).at[hot_flat].add(hot_terms)
    hot_grad = lax.psum_scatter(hot_sums, ("wide", "narrow"), scatter_dimension=0, tiled=True)
    proj_sum, out_sum, gain_sum = totals
    proj_sum, out_sum, gain_sum = lax.psum((proj_sum, out_sum, gain_sum), "narrow")
    proj_sum, out_sum, gain_sum = (
        lax.psum_scatter(proj_sum, "wide", scatter_dimension=1, tiled=True),
        lax.psum_scatter(out_sum, "wide", scatter_dimension=1, tiled=True),
        lax.psum_scatter(gain_sum, "wide", scatter_dimension=1, tiled=True),
    )
    return (proj_sum, out_sum, gain_sum, cold_grad, hot_grad)


def solution(mesh):
    in_specs = (
        P(("wide", "narrow"), None, None),
        P(("wide", "narrow"), None),
        P(("wide", "narrow"), None),
        P(("wide", "narrow"), None),
        P(("wide", "narrow")),
        P("wide", None),
        P(),
        P(),
        P(),
        P(),
        P(("wide", "narrow"), None, None),
    )
    out_specs = (
        P(None, "wide"),
        P(None, "wide"),
        P(None, "wide"),
        P(("wide", "narrow"), None),
        P(("wide", "narrow"), None),
    )
    return jax.shard_map(local, mesh=mesh, in_specs=in_specs, out_specs=out_specs, check_vma=False)
```

profile of v0, /device:TPU:1, one launch (start us, length us, event | category | flops | bytes accessed | tf_op | source)
XLA Modules:
  0.0 529.0 jit_solution(10135026107503968535)
XLA Ops:
  10.2 18.0 %reduce-window.6 = s32[64,8,128]{2,1,0:T(8,128)S(1)} reduce-window(s32[64,8,128]{2,1,0:T(8,128)S(1)} %fusion.47, s32[]{:T(128)} %constant.28.clone.1), window={size=1x1x128 pad=0_0x0_0x127_0}, to_apply=%region_0.0 | reduce-window | flops 8323072 | bytes 524292 | tf_op jit(solution)/shard_map/reduce-window
  28.9 4.3 scatter_custom_fusion
  33.3 22.2 %all_to_all.22 = s32[64,1,24]{2,1,0:T(1,128)S(1)} all-to-all(s32[64,1,24]{2,1,0:T(1,128)S(1)} %bitcast.255), channel_id=1, replica_groups=mesh['wide'=64,'narrow'=4] {'wide'}, dimensions={0} | all-to-all | bytes 12288 | tf_op jit(solution)/shard_map/all_to_all | solution.py:98
  56.3 5.4 %gather_fusion.1 = bf16[1536,512]{1,0:T(8,128)(2,1)} fusion(bf16[1024,512]{1,0:T(8,128)(2,1)S(1)} %copy-done, s32[2048]{0:T(1024)S(1)} %pad_clamp_fusion), kind=kCustom, calls=%fused_computation.1 | custom fusion | bytes 3151872 | tf_op jit(solution)/shard_map/gather | solution.py:99
  61.7 4.9 all-to-all-start.1
  66.8 5.0 gather_fusion
  71.8 2.3 copy.54
  74.2 32.3 %all-to-all-done.1 = bf16[64,24,512]{2,1,0:T(8,128)(2,1)S(1)} async-done(((bf16[64,24,512]{2,1,0:T(8,128)(2,1)}), bf16[64,24,512]{2,1,0:T(8,128)(2,1)S(1)}, u32[]{:S(2)}, u32[]{:S(2)}) %all-to-all-start.1) | async-done | bytes 1572896 | tf_op jit(solution)/shard_map/all_to_all | solution.py:100
  106.5 4.0 gather_fusion.2
  112.3 61.6 %while.17 = (s32[]{:T(128)}, f32[512,2048]{1,0:T(8,128)}, f32[512,512]{1,0:T(8,128)}, f32[1,512]{1,0:T(1,128)S(1)}, bf16[2,512,512]{2,1,0:T(8,128)(2,1)}, /*inde...) while((s32[]{:T(128)}, f32[512,2048]{1,0:T(8,128)}, ...), condition=%wide.region_14.15_spmd.clone, body=%wide.region_4.14_spmd.clone.sunk | while | flops 5443427840 | bytes 113894808 | solution.py:117
  116.0 3.7 multiply_convert_fusion.5
  124.0 2.5 fusion.138
  128.3 1.8 fusion.141
  134.8 2.0 copy.77
  136.8 1.9 constant_dynamic-update-slice_fusion.2
  138.8 3.3 select_add_fusion.2
  145.7 3.7 multiply_convert_fusion.5
  153.7 2.5 fusion.138
  158.0 1.8 fusion.141
  164.5 2.0 copy.77
  166.6 1.9 constant_dynamic-update-slice_fusion.2
  168.5 5.5 %select_add_fusion.2 = f32[512,2048]{1,0:T(8,128)} fusion(f32[512,2048]{1,0:T(8,128)} %get-tuple-element.310, bf16[512,2048]{0,1:T(8,128)(2,1)S(1)} %fusion.141, pred[]{:T(512)S(6)} %compare.7, f32[512]{0:T(512)S(1)} %bitcast.252, f32[512]{0:T(512)S(1)} %fusion.131, f32[512]{0:T(512)S(1)} %broadcast_multiply_fusion.5, ...), kind=kOutput, calls=%fused_computation.17.clone.1 | convolution fusion | flops 1077149696 | bytes 11016197 | tf_op jit(solution)/shard_map/while/body/eval_jaxpr/dot_general | solution.py:59
  174.0 5.3 %copy.57 = f32[512,2048]{0,1:T(8,128)} copy(f32[512,2048]{1,0:T(8,128)} %get-tuple-element.65) | data formatting | bytes 8388608 | tf_op jit(solution)/shard_map/while | solution.py:117
  180.8 6.6 %scatter_custom_fusion.1 = bf16[1536,512]{1,0:T(8,128)(2,1)} fusion(s32[1024]{0:T(1024)} %bitcast.261, bf16[1024,512]{1,0:T(8,128)(2,1)S(1)} %bitcast_select_fusion, bf16[]{:T(256)} %constant.32.clone.1), kind=kCustom, calls=%fused_computation.89 | custom fusion | bytes 1573376 | tf_op jit(solution)/shard_map/scatter | solution.py:123
  187.3 6.2 %all-to-all-start.2 = ((bf16[64,24,512]{2,1,0:T(8,128)(2,1)}), bf16[64,24,512]{2,1,0:T(8,128)(2,1)S(1)}, u32[]{:S(2)}, u32[]{:S(2)}) async-start(bf16[64,24,512]{2,1,0:T(8,128)(2,1)} %bitcast.15), calls=%async_computation.2 | async-start | bytes 3145728 | tf_op jit(solution)/shard_map/all_to_all | solution.py:126
  195.2 8.8 %scatter_custom_fusion.3 = f32[1024,512]{1,0:T(8,128)} fusion(s32[1024]{0:T(1024)} %bitcast.265, f32[1024,512]{1,0:T(8,128)} %convert_select_fusion, f32[]{:T(128)} %constant.30.clone.1), kind=kCustom, calls=%fused_computation.85 | custom fusion | flops 524288 | bytes 2097664 | tf_op jit(solution)/shard_map/scatter-add | solution.py:134
  206.9 108.5 %reduce-scatter.7.cloned.1.call-done = f32[512,32]{0,1:T(8,128)} async-done(((f32[512,2048]{0,1:T(8,128)}), f32[512,32]{0,1:T(8,128)}) %reduce-scatter.7.cloned.1.call-update) | async-done | bytes 65552 | tf_op jit(solution)/shard_map/reduce_scatter | solution.py:139
  315.5 11.2 %scatter_custom_fusion.2 = f32[1024,512]{1,0:T(8,128)} fusion(s32[1536]{0:T(1024)S(1)} %fusion.48, bf16[1536,512]{1,0:T(8,128)(2,1)S(1)} %bitcast.244, f32[]{:T(128)} %constant.30.clone.1), kind=kCustom, calls=%fused_computation.81 | custom fusion | flops 1572864 | bytes 3670020 | tf_op jit(solution)/shard_map/scatter-add | solution.py:130
  328.0 129.2 %all-reduce.4 = f32[1,512]{1,0:T(1,128)S(1)} all-reduce(f32[1,512]{1,0:T(1,128)S(1)} %get-tuple-element.67), channel_id=4, replica_groups=mesh['wide'=64,'narrow'=4] {'wide'}, use_global_device_ids=true, to_apply=%region_20.21.clone | all-reduce | flops 512 | bytes 4096
  457.2 12.8 %all-reduce.12.cloned.1.call-done = f32[1024,512]{1,0:T(8,128)} async-done(((f32[1024,512]{1,0:T(8,128)}), f32[1024,512]{1,0:T(8,128)}) %all-reduce.12.cloned.1.call-update) | async-done | bytes 2097168
  471.4 15.0 %all-reduce.6 = (f32[512,8]{0,1:T(8,128)}, f32[1,8]{1,0:T(1,128)}) all-reduce(f32[512,8]{0,1:T(8,128)} %reduce-scatter.9.cloned.1.call-done, f32[1,8]{1,0:T(1,128)S(1)} %constant_dynamic-slice_fusion.2), channel_id=1, replica_groups=mesh['wide'=64,'narrow'=4] {'narrow'}, use_global_device_ids=true, to_apply=%region_17.18 | all-reduce | flops 4104 | bytes 32832 | tf_op jit(solution)/shard_map/psum | solution.py:137
  486.4 34.0 %all-reduce.10.cloned.1.call-done = f32[512,32]{0,1:T(8,128)} async-done(((f32[512,32]{0,1:T(8,128)}), f32[512,32]{0,1:T(8,128)}) %all-reduce.10.cloned.1.call-update) | async-done | bytes 65552 | tf_op jit(solution)/shard_map/psum | solution.py:137
  (170 shorter events, 42.2 us)
Async XLA Ops:
  8.0 48.3 %copy-start = (bf16[1024,512]{1,0:T(8,128)(2,1)S(1)}, bf16[1024,512]{1,0:T(8,128)(2,1)}, u32[]{:S(2)}) copy-start(bf16[1024,512]{1,0:T(8,128)(2,1)} %param.18) | copy-start | bytes 3145732
  8.0 20.8 %copy-start.13 = (s32[2,512,1]{1,2,0:T(1,128)S(1)}, s32[2,512,1]{1,2,0:T(1,128)}, u32[]{:S(2)}) copy-start(s32[2,512,1]{1,2,0:T(1,128)} %param.13) | copy-start | bytes 12292
  28.9 45.3 %copy-start.16 = (s32[1024,1]{0,1:T(1,128)}, s32[1024,1]{0,1:T(1,128)S(1)}, u32[]{:S(2)}) copy-start(s32[1024,1]{0,1:T(1,128)S(1)} %compare_select_fusion.2) | copy-start | bytes 12292
  61.7 5.0 copy-start.19
  61.7 5.1 copy-start.4
  61.7 44.7 %all-to-all-start.1 = ((bf16[64,24,512]{2,1,0:T(8,128)(2,1)}), bf16[64,24,512]{2,1,0:T(8,128)(2,1)S(1)}, u32[]{:S(2)}, u32[]{:S(2)}) async-start(bf16[64,24,512]{2,1,0:T(8,128)(2,1)} %bitcast.243), calls=%async_computation.1 | async-start | bytes 3145728 | tf_op jit(solution)/shard_map/all_to_all | solution.py:100
  66.6 248.7 %reduce-scatter.7.cloned.1.call-start = ((), (), s32[]{:S(2)}) async-start(), calls=%async_computation.7 | async-start | bytes 4259840 | tf_op jit(solution)/shard_map/reduce_scatter | solution.py:139
  66.7 5.1 copy-start.17
  71.8 2.3 copy-start.18
  74.1 36.8 %copy-start.14 = (pred[2,512]{1,0:T(4,128)(4,1)}, pred[2,512]{1,0:T(4,128)(4,1)S(1)}, u32[]{:S(2)}) copy-start(pred[2,512]{1,0:T(4,128)(4,1)S(1)} %broadcast_compare_fusion) | copy-start | bytes 3076
  110.4 1.2 copy-start.9
  115.9 6.7 %copy-start.2 = (bf16[1,512,512]{1,2,0:T(8,128)(2,1)}, bf16[1,512,512]{1,2,0:T(8,128)(2,1)S(1)}, u32[]{:S(2)}) copy-start(bf16[1,512,512]{1,2,0:T(8,128)(2,1)S(1)} %copy.76) | copy-start | bytes 1572868 | tf_op jit(solution)/shard_map/while
  121.6 1.0 copy-start.21
  128.3 1.8 copy-start.3
  128.3 1.8 copy-start.5
  130.1 1.6 copy-start.20
  131.7 1.3 copy-start.6
  145.6 6.7 %copy-start.2 = (bf16[1,512,512]{1,2,0:T(8,128)(2,1)}, bf16[1,512,512]{1,2,0:T(8,128)(2,1)S(1)}, u32[]{:S(2)}) copy-start(bf16[1,512,512]{1,2,0:T(8,128)(2,1)S(1)} %copy.76) | copy-start | bytes 1572868 | tf_op jit(solution)/shard_map/while
  158.0 1.8 copy-start.3
  158.0 1.8 copy-start.5
  159.8 1.6 copy-start.20
  161.4 1.3 copy-start.6
  179.3 1.2 copy-start.8
  187.3 128.1 %all-to-all-start.2 = ((bf16[64,24,512]{2,1,0:T(8,128)(2,1)}), bf16[64,24,512]{2,1,0:T(8,128)(2,1)S(1)}, u32[]{:S(2)}, u32[]{:S(2)}) async-start(bf16[64,24,512]{2,1,0:T(8,128)(2,1)} %bitcast.15), calls=%async_computation.2 | async-start | bytes 3145728 | tf_op jit(solution)/shard_map/all_to_all | solution.py:126
  193.6 276.5 %all-reduce.12.cloned.1.call-start = ((), (), s32[]{:S(2)}) async-start(), calls=%async_computation.10 | async-start | bytes 4194304
  195.2 8.9 %copy-start.7 = (f32[512,512]{1,0:T(8,128)S(1)}, f32[512,512]{1,0:T(8,128)}, u32[]{:S(2)}) copy-start(f32[512,512]{1,0:T(8,128)} %get-tuple-element.66) | copy-start | bytes 3145732
  204.0 2.0 copy-start.12
  204.0 267.4 %reduce-scatter.9.cloned.1.call-start = ((), (), s32[]{:S(2)}) async-start(), calls=%async_computation.9 | async-start | bytes 1064960 | tf_op jit(solution)/shard_map/reduce_scatter | solution.py:140
  205.5 314.9 %all-reduce.10.cloned.1.call-start = ((), (), s32[]{:S(2)}) async-start(), calls=%async_computation.8 | async-start | bytes 131072 | tf_op jit(solution)/shard_map/psum | solution.py:137
  315.4 205.0 %reduce-scatter.5.cloned.1.call-start = ((), (), s32[]{:S(2)}) async-start(), calls=%async_computation.6 | async-start | bytes 2621440 | tf_op jit(solution)/shard_map/reduce_scatter | solution.py:132
  315.5 206.4 %copy-start.1 = (bf16[1024,512]{1,0:T(8,128)(2,1)S(1)}, bf16[1024,512]{1,0:T(8,128)(2,1)}, u32[]{:S(2)}) copy-start(bf16[1024,512]{1,0:T(8,128)(2,1)} %param.18) | copy-start | bytes 3145732
  315.5 11.3 %copy-start.23 = (u32[256]{0:T(256)S(1)}, u32[256]{0:T(256)}, u32[]{:S(2)}) copy-start(u32[256]{0:T(256)} %constant.83) | copy-start | bytes 3076
  (5 other events, 3.6 us)
Sparse Core Ops, SparseCore 0:
  179.5 135.8 reduce-scatter.6
  319.3 138.3 reduce-scatter.8
  460.9 35.5 reduce-scatter.4
Sparse Core Ops, SparseCore 1:
  204.1 265.9 all-reduce.11
  472.3 48.0 all-reduce.9
where the time goes:
time: 531 us; the launch traced here: 529 us
  waiting for transfers between devices  188 us (35%)
  blocking collectives  166 us (31%)
  local copies, waits for them, and re-layouts  57.3 us (11%)
  other arithmetic  53.7 us (10%)
  matrix products  34.5 us (6%)
  between operations  16.2 us (3%)
  starting transfers between devices  11.3 us (2%)
    unnamed x1, blocking collectives  129 us
    reduce_scatter x1, waiting for transfers between devices, local(): lax.psum_scatter(proj_sum, 'wide', scatter_dimension=1, tiled=True)  108 us
    psum x1, waiting for transfers between devices, local(): lax.psum((proj_sum, out_sum, gain_sum), 'narrow')  34 us
    all_to_all x1, waiting for transfers between devices, local(): lax.all_to_all(found, 'wide', split_axis=0, concat_axis=0, tiled=True)  32.3 us
    all_to_all x1, blocking collectives, local(): lax.all_to_all(request, 'wide', split_axis=0, concat_axis=0, tiled=True)  22.2 us
    another operation x3, other arithmetic  18.2 us
    psum x1, blocking collectives, local(): lax.psum((proj_sum, out_sum, gain_sum), 'narrow')  15 us
    unnamed x6, waiting for transfers between devices  12.9 us
  transfers between devices with their start and end apart: 7, of which 4 were waited for; matrix products, arithmetic and copies ran while one was open for 8% of the time, Pallas kernels for 0%

commit v1 on v0

v1 whole, which is shorter than its diff:
```python
import functools

import jax
import jax.numpy as jnp
from jax import lax
from jax.experimental import pallas as pl
from jax.experimental.pallas import tpu as pltpu
from jax.sharding import PartitionSpec as P

WIDE = 64
NARROW = 4
CAP = 24
TOK = 1024
LEN = 512
D = 512
HEADS = 4
ROWS = 1024
EPS = 1e-05
SCALE = 128 ** (-0.5)
MESH = pl.DeviceIdType.MESH
F32 = jnp.float32
BF16 = jnp.bfloat16


def mm(a, b):
    return jnp.dot(a, b, preferred_element_type=F32)


def mm_nt(a, b):
    return lax.dot_general(a, b, (((1,), (1,)), ((), ())), preferred_element_type=F32)


def mm_tn(a, b):
    return lax.dot_general(a, b, (((0,), (0,)), ((), ())), preferred_element_type=F32)


def iota(shape, dim):
    return lax.broadcasted_iota(jnp.int32, shape, dim).astype(F32)


def sigmoid(x):
    return 0.5 * jnp.tanh(0.5 * x) + 0.5


def onehot(mask):
    return jnp.where(mask, 1.0, 0.0).astype(BF16)


def mean(x):
    return jnp.mean(x, axis=-1, keepdims=True)


def pack(rows):
    blocks = rows.reshape(-1, CAP, D)
    return jnp.concatenate([blocks[:, :, : D // 2], blocks[:, :, D // 2 :]], axis=1).astype(BF16)


def unpack_into(dst, src):
    def step(i, carry):
        block = src[pl.ds(i * 8, 8)].astype(F32)
        rows = pl.ds(pl.multiple_of(i * 192, 192), 192)
        dst[rows, : D // 2] = block[:, :CAP].reshape(192, D // 2).astype(BF16)
        dst[rows, D // 2 :] = block[:, CAP:].reshape(192, D // 2).astype(BF16)
        return carry

    lax.fori_loop(0, 8, step, 0)


def kernel(
    tok, lens, table, hot_table, weight, out_weight, gain, cot,
    proj_out, out_out, gain_out, cold_out, hot_out,
    slots, req, want, reply, got, rows_in, place_t, hot_t, emb, normed, xhat, spread, acted, dact,
    attn, dattn, per_head, mixed, masked, mixed_cot, dhead, proj_cot, emb_grad, gain_sum,
    cold_send, cold_got, wsum, core_got, core_sum, x_got, x_sum, y_got, y_sum, z_got, gathered, cx_send, cx_got,
    loc_sem, a2a_send, a2a_recv, core_ss, core_rs, x_ss, x_rs, y_ss, y_rs, z_ss, z_rs, g_ss, g_rs, cx_ss, cx_rs,
):
    w = lax.axis_index("wide")
    n = lax.axis_index("narrow")
    core = lax.rem(w, 2)
    chip = lax.div(w, 2)
    z = lax.rem(chip, 8)
    y = lax.div(chip, 8)

    barrier = pltpu.get_barrier_semaphore()

    def greet(d, carry):
        pl.semaphore_signal(barrier, inc=1, device_id=(lax.rem(w + d, WIDE), n), device_id_type=MESH)
        return carry

    lax.fori_loop(1, WIDE, greet, 0)
    for d in range(1, NARROW):
        pl.semaphore_signal(barrier, inc=1, device_id=(w, lax.rem(n + d, NARROW)), device_id_type=MESH)

    upper = onehot(iota((128, 128), 0) < iota((128, 128), 1))
    sub = iota((128, 128), 0)
    carry = jnp.zeros((128, 1), F32)
    req_hi = jnp.zeros((128, 128), F32)
    req_lo = jnp.zeros((128, 128), F32)
    for a in range(8):
        own = tok[a : a + 1, :]
        row = tok[8 + a : 9 + a, :]
        hot = tok[16 + a : 17 + a, :]
        owns = jnp.where(sub == own, 1.0, 0.0)
        owns_b = owns.astype(BF16)
        before = mm(owns_b, upper) + carry
        rank = jnp.sum(owns * before, axis=0, keepdims=True)
        carry = carry + jnp.sum(owns, axis=1, keepdims=True)
        slots[a : a + 1, :] = jnp.where(hot >= 0.0, -1.0, own * CAP + rank)
        high = jnp.floor(row * (1.0 / 32.0))
        low = row - 32.0 * high
        ranked = sub == rank
        req_hi = req_hi + mm_nt(owns_b, jnp.where(ranked, high, 0.0).astype(BF16))
        req_lo = req_lo + mm_nt(owns_b, jnp.where(ranked, low, 0.0).astype(BF16))
    asked = 32.0 * req_hi + req_lo
    for o in range(WIDE):
        req[o] = asked[o : o + 1, :]

    pl.semaphore_wait(barrier, WIDE - 1 + NARROW - 1)

    def exchange(which, src, dst, p):
        return pltpu.make_async_remote_copy(
            src_ref=src.at[p], dst_ref=dst.at[w], send_sem=a2a_send.at[which], recv_sem=a2a_recv.at[which],
            device_id=(p, n), device_id_type=MESH,
        )

    def await_all(sem, ref):
        view = ref.at[pl.ds(0, WIDE - 1)]
        pltpu.make_async_copy(view, view, sem).wait()

    def ask(d, carry):
        exchange(0, req, want, lax.rem(w + d, WIDE)).start()
        return carry

    lax.fori_loop(1, WIDE, ask, 0)
    own_want = pltpu.make_async_copy(req.at[w], want.at[w], loc_sem.at[0])
    own_want.start()

    def build_place(a, carry):
        rows = pl.ds(pl.multiple_of(a * 192, 192), 192)
        at = iota((192, 128), 0) + (a * 192).astype(F32)
        for b in range(8):
            place_t[rows, b * 128 : (b + 1) * 128] = onehot(at == slots[b : b + 1, :])
        return carry

    lax.fori_loop(0, 8, build_place, 0)

    def build_hot(a, carry):
        rows = pl.ds(pl.multiple_of(a * 128, 128), 128)
        at = iota((128, 128), 0) + (a * 128).astype(F32)
        for b in range(8):
            hot_t[rows, b * 128 : (b + 1) * 128] = onehot(at == tok[16 + b : 17 + b, :])
        return carry

    lax.fori_loop(0, 8, build_hot, 0)

    own_want.wait()
    await_all(a2a_recv.at[0], want)

    lanes = iota((CAP, ROWS), 1)

    def answer(i, carry):
        first = lax.rem(lax.div(w, 8) + i, 8) * 8
        asked8 = want[pl.ds(first, 8)].reshape(8, 128).T
        picks = jnp.concatenate([jnp.where(lanes == asked8[:CAP, j : j + 1], 1.0, 0.0) for j in range(8)], axis=0)
        reply[pl.ds(first, 8)] = pack(mm(picks.astype(BF16), table[...]))
        for j in range(8):
            p = first + j

            @pl.when(p != w)
            def _():
                exchange(1, reply, got, p).start()

        return carry

    lax.fori_loop(0, 8, answer, 0)
    own_reply = pltpu.make_async_copy(reply.at[w], got.at[w], loc_sem.at[1])
    own_reply.start()

    tok_cols = tok[...].T
    for half in range(2):
        rows = slice(half * LEN, (half + 1) * LEN)
        hots = jnp.concatenate(
            [onehot(iota((128, TOK), 1) == tok_cols[:, 16 + a : 17 + a]) for a in range(half * 4, half * 4 + 4)], axis=0
        )
        emb[rows, :] = mm(hots, hot_table[...]).astype(BF16)
        live = iota((LEN, 1), 0) < lens[half].astype(F32)
        masked[rows, :] = jnp.where(live, cot[rows, :].astype(F32), 0.0).astype(BF16)
        mixed_cot[rows, :] = mm_nt(masked[rows, :], out_weight[...]).astype(BF16)

    own_reply.wait()
    await_all(a2a_recv.at[1], got)
    unpack_into(rows_in, got)
    slot_cols = slots[...].T
    for half in range(2):
        rows = slice(half * LEN, (half + 1) * LEN)
        picks = jnp.concatenate(
            [onehot(iota((128, WIDE * CAP), 1) == slot_cols[:, a : a + 1]) for a in range(half * 4, half * 4 + 4)], axis=0
        )
        emb[rows, :] = (mm(picks, rows_in[...]) + emb[rows, :].astype(F32)).astype(BF16)

    gain_sum[...] = jnp.zeros_like(gain_sum)

    def layer(s, carry):
        base = s * LEN
        rows = pl.ds(pl.multiple_of(base, LEN), LEN)
        length = lens[s].astype(F32)

        def norm(t, c):
            part = pl.ds(pl.multiple_of(base + t * 256, 256), 256)
            x = emb[part, :].astype(F32)
            center = x - mean(x)
            r = lax.rsqrt(mean(center * center) + EPS)
            hat = center * r
            xhat[part, :] = hat
            spread[part, :] = r
            normed[part, :] = (hat * gain[...]).astype(BF16)
            return c

        lax.fori_loop(0, 2, norm, 0)

        def project(cb, c):
            cols = pl.ds(pl.multiple_of(cb * 256, 256), 256)
            p = mm(normed[rows, :], weight[:, cols])
            sig = sigmoid(p)
            a = p * sig
            acted[:, cols] = a.astype(BF16)
            dact[:, cols] = sig + a * (1.0 - sig)
            return c

        lax.fori_loop(0, 8, project, 0)

        def cols_of(block, h):
            return pl.ds(pl.multiple_of(block * D + h * 128, 128), 128)

        def attend(h, c):
            for part in range(2):
                keys = 256 * (part + 1)
                at = slice(256 * part, 256 * part + 256)
                q = acted[at, cols_of(2, h)]
                k = acted[:keys, cols_of(3, h)]
                v = acted[:keys, cols_of(1, h)]
                scores = mm_nt(q, k) * SCALE
                sig = sigmoid(scores)
                a = scores * sig
                ii = iota((256, keys), 0) + 256.0 * part
                jj = iota((256, keys), 1)
                inverse = 1.0 / jnp.full((1, keys), length)
                allowed = jnp.where((jj <= ii) & (jj < length), inverse, 0.0)
                weights = (a * allowed).astype(BF16)
                attn[h, at, :keys] = weights
                dattn[h, at, :keys] = (sig + a * (1.0 - sig)) * (allowed * SCALE)
                per_head[at, pl.ds(pl.multiple_of(h * 128, 128), 128)] = mm(weights, v)
            return c

        lax.fori_loop(0, HEADS, attend, 0)

        def gate_step(t, c):
            part = pl.ds(pl.multiple_of(t * 256, 256), 256)
            whole = pl.ds(pl.multiple_of(base + t * 256, 256), 256)
            x = per_head[part, :]
            center = x - mean(x)
            r = lax.rsqrt(mean(center * center) + EPS)
            hat = center * r
            gate = acted[part, :D].astype(F32)
            g = mixed_cot[whole, :].astype(F32)
            mixed[whole, :] = (hat * gate).astype(BF16)
            dgate = (g * hat).astype(BF16).astype(F32)
            proj_cot[whole, :D] = (dgate * dact[part, :D]).astype(BF16)
            dhat = g * gate
            dhead[part, :] = (r * (dhat - mean(dhat) - hat * mean(dhat * hat))).astype(BF16)
            return c

        lax.fori_loop(0, 2, gate_step, 0)

        def attend_back(h, c):
            def put(block, at, to, grad):
                cols = cols_of(block, h)
                proj_cot[to, cols] = (grad.astype(BF16).astype(F32) * dact[at, cols]).astype(BF16)

            dks, dvs = [], []
            for part in range(2):
                keys = 256 * (part + 1)
                at = slice(256 * part, 256 * part + 256)
                q = acted[at, cols_of(2, h)]
                k = acted[:keys, cols_of(3, h)]
                v = acted[:keys, cols_of(1, h)]
                do = dhead[at, pl.ds(pl.multiple_of(h * 128, 128), 128)]
                da = mm_nt(do, v).astype(BF16).astype(F32)
                ds = (da * dattn[h, at, :keys]).astype(BF16)
                put(2, at, pl.ds(pl.multiple_of(base + 256 * part, 256), 256), mm(ds, k))
                dks.append(mm_tn(ds, q))
                dvs.append(mm_tn(attn[h, at, :keys], do))
            for block, grads in ((3, dks), (1, dvs)):
                put(block, slice(0, 256), pl.ds(pl.multiple_of(base, 256), 256), grads[0] + grads[1][:256])
                put(block, slice(256, 512), pl.ds(pl.multiple_of(base + 256, 256), 256), grads[1][256:])
            return c

        lax.fori_loop(0, HEADS, attend_back, 0)

        def norm_back(t, c):
            part = pl.ds(pl.multiple_of(base + t * 256, 256), 256)
            ncot = mm_nt(proj_cot[part, :], weight[...])
            hat = xhat[part, :]
            gain_sum[...] += jnp.sum(ncot * hat, axis=0, keepdims=True)
            d = ncot * gain[...]
            ecot = spread[part, :] * (d - mean(d) - hat * mean(d * hat))
            live = iota((256, 1), 0) + (t * 256).astype(F32) < length
            total = masked[part, :].astype(F32) + ecot
            emb_grad[part, :] = jnp.where(live, total, 0.0).astype(BF16)
            return c

        lax.fori_loop(0, 2, norm_back, 0)
        return carry

    lax.fori_loop(0, 2, layer, 0)

    def give(i, carry):
        first = lax.rem(lax.div(w, 8) + i, 8) * 8
        rows = pl.ds(pl.multiple_of(first * CAP, 192), 192)
        cold_send[pl.ds(first, 8)] = pack(mm(place_t[rows, :], emb_grad[...]))
        for j in range(8):
            p = first + j

            @pl.when(p != w)
            def _():
                exchange(2, cold_send, cold_got, p).start()

        return carry

    lax.fori_loop(0, 8, give, 0)
    own_cold = pltpu.make_async_copy(cold_send.at[w], cold_got.at[w], loc_sem.at[2])
    own_cold.start()

    def weight_grad(cb, carry):
        grad = mm_tn(proj_cot[:, pl.ds(pl.multiple_of(cb * D, D), D)], normed[...])
        wsum[pl.ds(cb * 8, 8), :, 0:2] = grad.reshape(8, 2, 2, 16, D).astype(BF16)
        return carry

    lax.fori_loop(0, 4, weight_grad, 0)
    out_grad = mm_tn(masked[...], mixed[...]).reshape(WIDE, 8, D)
    gains = jnp.broadcast_to(gain_sum[...].reshape(1, 1, D), (WIDE, 8, D))
    wsum[:, :, 2] = jnp.concatenate([out_grad, gains], axis=1).reshape(32, 2, 16, D).astype(BF16)
    wsum[:, :, 3] = mm(hot_t[...], emb_grad[...]).reshape(32, 2, 16, D).astype(BF16)

    peer = w + 1 - 2 * core

    def core_copy(d):
        part = lax.rem(n + d, NARROW)
        return pltpu.make_async_remote_copy(
            src_ref=wsum.at[:, 1 - core, part], dst_ref=core_got.at[part], send_sem=core_ss.at[d], recv_sem=core_rs.at[d],
            device_id=(peer, n), device_id_type=MESH,
        )

    def x_copy(d):
        part = lax.rem(n + d, NARROW)
        return pltpu.make_async_remote_copy(
            src_ref=core_sum.at[part], dst_ref=x_got.at[d - 1], send_sem=x_ss.at[d - 1], recv_sem=x_rs.at[d - 1],
            device_id=(w, part), device_id_type=MESH,
        )

    order = (2, 1, 3, 0)
    for d in order:
        core_copy(d).start()
    for d in order:
        core_copy(d).wait_recv()
        part = lax.rem(n + d, NARROW)
        core_sum[part] = (wsum[:, core, part].astype(F32) + core_got[part].astype(F32)).astype(BF16)
        if d:
            x_copy(d).start()
    total = core_sum[n].astype(F32)
    for d in (1, 3, 2):
        x_copy(d).wait_recv()
        total = total + x_got[d - 1].astype(F32)
    x_sum[...] = total.astype(BF16).reshape(4, 8, 16, D)

    def y_copy(d):
        to = lax.rem(y + d, 4)
        return pltpu.make_async_remote_copy(
            src_ref=x_sum.at[to], dst_ref=y_got.at[d - 1], send_sem=y_ss.at[d - 1], recv_sem=y_rs.at[d - 1],
            device_id=((to * 8 + z) * 2 + core, n), device_id_type=MESH,
        )

    def z_copy(d):
        to = lax.rem(z + d, 8)
        return pltpu.make_async_remote_copy(
            src_ref=y_sum.at[to], dst_ref=z_got.at[d - 1], send_sem=z_ss.at[d - 1], recv_sem=z_rs.at[d - 1],
            device_id=((y * 8 + to) * 2 + core, n), device_id_type=MESH,
        )

    def g_copy(d):
        to = lax.rem(n + d, NARROW)
        return pltpu.make_async_remote_copy(
            src_ref=gathered.at[n], dst_ref=gathered.at[n], send_sem=g_ss.at[d - 1], recv_sem=g_rs.at[d - 1],
            device_id=(w, to), device_id_type=MESH,
        )

    def cx_copy(d):
        to = lax.rem(n + d, NARROW)
        return pltpu.make_async_remote_copy(
            src_ref=cx_send.at[d - 1], dst_ref=cx_got.at[d - 1], send_sem=cx_ss.at[d - 1], recv_sem=cx_rs.at[d - 1],
            device_id=(w, to), device_id_type=MESH,
        )

    for d in (2, 1, 3):
        y_copy(d).start()
    total = x_sum[y].astype(F32)
    for d in (1, 3, 2):
        y_copy(d).wait_recv()
        total = total + y_got[d - 1].astype(F32)
    y_sum[...] = total.astype(BF16)
    for d in range(1, 8):
        z_copy(d).start()
    total = y_sum[z].astype(F32)
    for d in range(1, 8):
        z_copy(d).wait_recv()
        total = total + z_got[d - 1].astype(F32)
    gathered[n] = total
    for d in range(1, NARROW):
        g_copy(d).start()

    asked = want[...].reshape(WIDE, 128)
    high = jnp.floor(asked * (1.0 / 32.0))
    low = asked - 32.0 * high
    line = iota((128, WIDE * CAP), 1)
    within = line - CAP * jnp.floor((line + 0.5) * (1.0 / CAP))
    spot = onehot(within == iota((128, WIDE * CAP), 0))
    spread_out = 32.0 * mm(high.astype(BF16), spot) + mm(low.astype(BF16), spot)
    line64 = iota((WIDE, WIDE * CAP), 1)
    start = iota((WIDE, WIDE * CAP), 0) * CAP
    mine = (line64 >= start) & (line64 < start + CAP)
    asked_line = jnp.sum(jnp.where(mine, spread_out, 0.0), axis=0, keepdims=True)

    own_cold.wait()
    await_all(a2a_recv.at[2], cold_got)
    unpack_into(rows_in, cold_got)

    def quarter(part):
        at = iota((256, WIDE * CAP), 0) + (part * 256).astype(F32)
        return mm(onehot(at == asked_line), rows_in[...])

    for d in (2, 1, 3):
        cx_send[d - 1] = quarter(lax.rem(n + d, NARROW)).astype(BF16)
        cx_copy(d).start()
    cold_out[...] = quarter(n)

    for d in range(1, NARROW):
        g_copy(d).wait_recv()
    proj_out[...] = gathered[0:2].reshape(32, D).T
    out_out[...] = gathered[2, 0:8].T
    gain_out[...] = gathered[2, 8:9]
    for k in range(NARROW):

        @pl.when(n == k)
        def _():
            hot_out[...] = gathered[3, 4 * k : 4 * k + 4]

    for d in (1, 3, 2):
        cx_copy(d).wait_recv()
        cold_out[...] += cx_got[d - 1].astype(F32)

    await_all(a2a_send.at[0], req)
    await_all(a2a_send.at[1], reply)
    await_all(a2a_send.at[2], cold_send)
    for d in range(NARROW):
        core_copy(d).wait_send()
    for d in range(1, NARROW):
        x_copy(d).wait_send()
        y_copy(d).wait_send()
        g_copy(d).wait_send()
        cx_copy(d).wait_send()
    for d in range(1, 8):
        z_copy(d).wait_send()


def local(
    item_owner, item_row, hot_row, hot_flag, seq_length, cold_table, hot_table, proj_weight, out_weight, norm_gain, cotangent
):
    hot_id = jnp.where(hot_flag == 1, hot_row, -1)
    tok = jnp.concatenate([a.reshape(8, 128) for a in (item_owner, item_row, hot_id)], axis=0).astype(F32)
    tok = jnp.concatenate([tok, jnp.zeros((8, 128), F32)], axis=0)
    vm = pl.BlockSpec(memory_space=pltpu.VMEM)
    sm = pl.BlockSpec(memory_space=pltpu.SMEM)
    v = pltpu.VMEM
    dma = pltpu.SemaphoreType.DMA
    slots = WIDE * CAP
    block = (WIDE, 48, 256)
    scratch = [
        v((8, 128), F32), v((WIDE, 1, 128), F32), v((WIDE, 1, 128), F32),
        v(block, BF16), v(block, BF16), v((slots, D), BF16), v((slots, TOK), BF16), v((TOK, TOK), BF16),
        v((TOK, D), BF16), v((TOK, D), BF16), v((TOK, D), F32), v((TOK, 1), F32),
        v((LEN, 4 * D), BF16), v((LEN, 4 * D), F32), v((HEADS, LEN, LEN), BF16), v((HEADS, LEN, LEN), F32),
        v((LEN, D), F32), v((TOK, D), BF16), v((TOK, D), BF16), v((TOK, D), BF16), v((LEN, D), BF16),
        v((TOK, 4 * D), BF16), v((TOK, D), BF16), v((1, D), F32),
        v(block, BF16), v(block, BF16),
        v((32, 2, 4, 16, D), BF16), v((4, 32, 16, D), BF16), v((4, 32, 16, D), BF16), v((3, 32, 16, D), BF16),
        v((4, 8, 16, D), BF16), v((3, 8, 16, D), BF16), v((8, 16, D), BF16), v((7, 16, D), BF16), v((4, 16, D), F32),
        v((3, 256, D), BF16), v((3, 256, D), BF16),
        dma((3,)), dma((3,)), dma((3,)), dma((4,)), dma((4,)), dma((3,)), dma((3,)), dma((3,)), dma((3,)),
        dma((7,)), dma((7,)), dma((3,)), dma((3,)), dma((3,)), dma((3,)),
    ]
    out_shape = [
        jax.ShapeDtypeStruct((D, 32), F32), jax.ShapeDtypeStruct((D, 8), F32), jax.ShapeDtypeStruct((1, D), F32),
        jax.ShapeDtypeStruct((256, D), F32), jax.ShapeDtypeStruct((4, D), F32),
    ]
    proj, out, gain, cold, hot = pl.pallas_call(
        kernel,
        out_shape=out_shape,
        in_specs=[vm, sm] + [vm] * 6,
        out_specs=[vm] * 5,
        scratch_shapes=scratch,
        compiler_params=pltpu.CompilerParams(collective_id=0, has_side_effects=True, vmem_limit_bytes=62 * 1024 * 1024),
    )(tok, seq_length, cold_table, hot_table, proj_weight, out_weight, norm_gain, cotangent.reshape(TOK, D))
    gain = lax.dynamic_slice(gain, (0, lax.axis_index("wide") * 8), (1, 8))
    return proj, out, gain, cold, hot


def solution(mesh):
    both = P(("wide", "narrow"))
    in_specs = (both, both, both, both, both, P("wide"), P(), P(), P(), P(), both)
    out_specs = (P(None, "wide"), P(None, "wide"), P(None, "wide"), both, both)
    return jax.shard_map(local, mesh=mesh, in_specs=in_specs, out_specs=out_specs, check_vma=False)
```

time: 531 us -> 162 us (0.31)
  waiting for transfers between devices: 188 us -> 0 us
  blocking collectives: 166 us -> 0 us
  Pallas kernels: 0 us -> 151 us
  other arithmetic: 53.7 us -> 1.4 us
  local copies, waits for them, and re-layouts: 57.3 us -> 9.03 us
  matrix products: 34.5 us -> 0 us
  between operations: 16.2 us -> 0.65 us
  starting transfers between devices: 11.3 us -> 0 us
    pallas_call x0 -> x1, Pallas kernels: none -> 151 us  [local(): pl.pallas_call(kernel, out_shape=out_shape, in_specs=[vm, sm] + [vm] * 6,...]
    unnamed x1 -> x0, blocking collectives: 129 us -> none
    reduce_scatter x3 -> x0, waiting for transfers between devices: 108 us -> none  [the longest x1 108 us: local(): lax.psum_scatter(proj_sum, 'wide', scatter_dimension=1, tiled=True)]
    dot_general x22 -> x0, matrix products: 34.5 us -> none  [the longest x2 8.74 us: layer_grads(): proj_part = jnp.dot(normed.T, proj_cot, preferred_element_type=jnp.float32)]
    psum x1 -> x0, waiting for transfers between devices: 34 us -> none  [local(): lax.psum((proj_sum, out_sum, gain_sum), 'narrow')]
    all_to_all x2 -> x0, waiting for transfers between devices: 32.3 us -> none  [the longest x1 32.3 us: local(): lax.all_to_all(found, 'wide', split_axis=0, concat_axis=0, tiled=True)]
    all_to_all x1 -> x0, blocking collectives: 22.2 us -> none  [local(): lax.all_to_all(request, 'wide', split_axis=0, concat_axis=0, tiled=True)]
    scatter-add x2 -> x0, other arithmetic: 20 us -> none  [the longest x1 11.2 us: local(): row_sums = jnp.zeros((shard_rows, width), jnp.float32).at[wanted.reshape(...]
  transfers between devices with their start and end apart: 7 -> 0, of which waited for: 4 -> 0; matrix products, arithmetic and copies ran while one was open for 8% -> 0% of each run, Pallas kernels for 0% -> 0%
where the time goes in v1:
time: 162 us
  Pallas kernels  151 us (93%)
  local copies, waits for them, and re-layouts  9.03 us (6%)
    pallas_call x1, Pallas kernels, local(): pl.pallas_call(kernel, out_shape=out_shape, in_specs=[vm, sm] + [vm] * 6,...  151 us
    unnamed x4, local copies, waits for them, and re-layouts  6.51 us

profile of v1, /device:TPU:1, one launch (start us, length us, event | category | flops | bytes accessed | tf_op | source)
XLA Modules:
  0.0 161.8 jit_solution(3416507707917388083)
XLA Ops:
  0.6 0.7 reshape.23
  1.3 0.7 compare_select_fusion
  2.1 0.7 add_convert_fusion
  2.7 0.6 concatenate.7.tok
  3.4 150.7 %shard_map.146 = (f32[512,32]{1,0:T(8,128)}, f32[512,8]{1,0:T(8,128)}, f32[1,512]{1,0:T(1,128)}, f32[256,512]{1,0:T(8,128)}, f32[4,512]{1,0:T(4,128)}) custom-call(f32[32,128]{1,0:T(8,128)} %concatenate.7.tok, s32[2]{0:T(128)} %lens.1, bf16[1024,512]{1,0:T(8,128)(2,1)} %table.1, bf16[1024,512]{1,0:T(8,128)(2,1)} %hot_table.1, bf16[512,2048]{1,0:T(8,128)(2,1)} %weight.1, ...), custom_call_target="tpu_custom_call" | custom-call | tf_op jit(solution)/shard_map/pallas_call | solution.py:505
  154.1 1.2 constant_dynamic-slice_fusion
  155.3 1.7 %copy.16 = f32[512,32]{0,1:T(8,128)} copy(f32[512,32]{1,0:T(8,128)} %get-tuple-element.15) | data formatting | bytes 131072
  157.0 1.7 %copy.17 = f32[512,8]{0,1:T(8,128)} copy(f32[512,8]{1,0:T(8,128)} %get-tuple-element.16) | data formatting | bytes 32768
  158.7 1.9 %copy.20 = f32[256,512]{1,0:T(8,128)} copy(f32[256,512]{1,0:T(8,128)} %get-tuple-element.28) | data formatting | bytes 1048576
  160.5 1.3 copy.21
  (1 shorter events, 0.0 us)

commit v2 on v1

--- a/solution.py
+++ b/solution.py
@@ -13,6 +13,7 @@
 TOK = 1024
 LEN = 512
 D = 512
+HALF = 256
 HEADS = 4
 ROWS = 1024
 EPS = 1e-05
@@ -51,28 +52,31 @@
 
 
 def pack(rows):
-    blocks = rows.reshape(-1, CAP, D)
-    return jnp.concatenate([blocks[:, :, : D // 2], blocks[:, :, D // 2 :]], axis=1).astype(BF16)
-
-
-def unpack_into(dst, src):
+    half = rows.shape[1] // 2
+    blocks = rows.reshape(-1, CAP, rows.shape[1])
+    return jnp.concatenate([blocks[:, :, :half], blocks[:, :, half:]], axis=1).astype(BF16)
+
+
+def unpack_into(dst, src, start=0):
+    half = src.shape[-1]
+
     def step(i, carry):
         block = src[pl.ds(i * 8, 8)].astype(F32)
         rows = pl.ds(pl.multiple_of(i * 192, 192), 192)
-        dst[rows, : D // 2] = block[:, :CAP].reshape(192, D // 2).astype(BF16)
-        dst[rows, D // 2 :] = block[:, CAP:].reshape(192, D // 2).astype(BF16)
+        dst[rows, start : start + half] = block[:, :CAP].reshape(192, half).astype(BF16)
+        dst[rows, start + half : start + 2 * half] = block[:, CAP:].reshape(192, half).astype(BF16)
         return carry
 
     lax.fori_loop(0, 8, step, 0)
 
 
 def kernel(
-    tok, lens, table, hot_table, weight, out_weight, gain, cot,
-    proj_out, out_out, gain_out, cold_out, hot_out,
-    slots, req, want, reply, got, rows_in, place_t, hot_t, emb, normed, xhat, spread, acted, dact,
+    owner, row_in, hot_row, hot_flag, lens, gain, table_in, hot_table_in, weight_in, out_weight_in, cot_in,
+    gathered_out, cold_own, cx_got,
+    table, hot_table, weight, out_weight, cot, tok, slots, req, want, reply, got, rows_in, place_t, hot_t, emb, normed, xhat, spread, acted, dact,
     attn, dattn, per_head, mixed, masked, mixed_cot, dhead, proj_cot, emb_grad, gain_sum,
-    cold_send, cold_got, wsum, core_got, core_sum, x_got, x_sum, y_got, y_sum, z_got, gathered, cx_send, cx_got,
-    loc_sem, a2a_send, a2a_recv, core_ss, core_rs, x_ss, x_rs, y_ss, y_rs, z_ss, z_rs, g_ss, g_rs, cx_ss, cx_rs,
+    cold_send, cold_got, wsum, core_got, core_sum, x_got, x_sum, y_got, y_sum, z_got, gathered, cx_send,
+    load_sem, loc_sem, a2a_send, a2a_recv, core_ss, core_rs, x_ss, x_rs, y_ss, y_rs, z_ss, z_rs, g_ss, g_rs, cx_ss, cx_rs,
 ):
     w = lax.axis_index("wide")
     n = lax.axis_index("narrow")
@@ -81,6 +85,15 @@
     z = lax.rem(chip, 8)
     y = lax.div(chip, 8)
 
+    loads = [
+        pltpu.make_async_copy(src, dst, load_sem.at[i])
+        for i, (src, dst) in enumerate(
+            [(table_in, table), (hot_table_in, hot_table), (cot_in, cot), (out_weight_in, out_weight), (weight_in, weight)]
+        )
+    ]
+    for load in loads:
+        load.start()
+
     barrier = pltpu.get_barrier_semaphore()
 
     def greet(d, carry):
@@ -90,6 +103,12 @@
     lax.fori_loop(1, WIDE, greet, 0)
     for d in range(1, NARROW):
         pl.semaphore_signal(barrier, inc=1, device_id=(w, lax.rem(n + d, NARROW)), device_id_type=MESH)
+
+    for a in range(8):
+        at = (slice(a // 4, a // 4 + 1), slice(a % 4 * 128, a % 4 * 128 + 128))
+        tok[a : a + 1, :] = owner[a // 4, :, at[1]].astype(F32)
+        tok[8 + a : 9 + a, :] = row_in[at].astype(F32)
+        tok[16 + a : 17 + a, :] = jnp.where(hot_flag[at] == 1, hot_row[at], -1).astype(F32)
 
     upper = onehot(iota((128, 128), 0) < iota((128, 128), 1))
     sub = iota((128, 128), 0)
@@ -154,6 +173,7 @@
     lax.fori_loop(0, 8, build_hot, 0)
 
     own_want.wait()
+    loads[0].wait()
     await_all(a2a_recv.at[0], want)
 
     lanes = iota((CAP, ROWS), 1)
@@ -176,6 +196,8 @@
     own_reply = pltpu.make_async_copy(reply.at[w], got.at[w], loc_sem.at[1])
     own_reply.start()
 
+    for load in loads[1:]:
+        load.wait()
     tok_cols = tok[...].T
     for half in range(2):
         rows = slice(half * LEN, (half + 1) * LEN)
@@ -207,12 +229,13 @@
 
         def norm(t, c):
             part = pl.ds(pl.multiple_of(base + t * 256, 256), 256)
+            here = pl.ds(pl.multiple_of(t * 256, 256), 256)
             x = emb[part, :].astype(F32)
             center = x - mean(x)
             r = lax.rsqrt(mean(center * center) + EPS)
             hat = center * r
-            xhat[part, :] = hat
-            spread[part, :] = r
+            xhat[here, :] = hat
+            spread[here, :] = r
             normed[part, :] = (hat * gain[...]).astype(BF16)
             return c
 
@@ -299,11 +322,12 @@
 
         def norm_back(t, c):
             part = pl.ds(pl.multiple_of(base + t * 256, 256), 256)
+            here = pl.ds(pl.multiple_of(t * 256, 256), 256)
             ncot = mm_nt(proj_cot[part, :], weight[...])
-            hat = xhat[part, :]
+            hat = xhat[here, :]
             gain_sum[...] += jnp.sum(ncot * hat, axis=0, keepdims=True)
             d = ncot * gain[...]
-            ecot = spread[part, :] * (d - mean(d) - hat * mean(d * hat))
+            ecot = spread[here, :] * (d - mean(d) - hat * mean(d * hat))
             live = iota((256, 1), 0) + (t * 256).astype(F32) < length
             total = masked[part, :].astype(F32) + ecot
             emb_grad[part, :] = jnp.where(live, total, 0.0).astype(BF16)
@@ -314,109 +338,143 @@
 
     lax.fori_loop(0, 2, layer, 0)
 
-    def give(i, carry):
-        first = lax.rem(lax.div(w, 8) + i, 8) * 8
-        rows = pl.ds(pl.multiple_of(first * CAP, 192), 192)
-        cold_send[pl.ds(first, 8)] = pack(mm(place_t[rows, :], emb_grad[...]))
-        for j in range(8):
-            p = first + j
-
-            @pl.when(p != w)
-            def _():
-                exchange(2, cold_send, cold_got, p).start()
-
-        return carry
-
-    lax.fori_loop(0, 8, give, 0)
-    own_cold = pltpu.make_async_copy(cold_send.at[w], cold_got.at[w], loc_sem.at[2])
-    own_cold.start()
-
-    def weight_grad(cb, carry):
-        grad = mm_tn(proj_cot[:, pl.ds(pl.multiple_of(cb * D, D), D)], normed[...])
-        wsum[pl.ds(cb * 8, 8), :, 0:2] = grad.reshape(8, 2, 2, 16, D).astype(BF16)
-        return carry
-
-    lax.fori_loop(0, 4, weight_grad, 0)
-    out_grad = mm_tn(masked[...], mixed[...]).reshape(WIDE, 8, D)
-    gains = jnp.broadcast_to(gain_sum[...].reshape(1, 1, D), (WIDE, 8, D))
-    wsum[:, :, 2] = jnp.concatenate([out_grad, gains], axis=1).reshape(32, 2, 16, D).astype(BF16)
-    wsum[:, :, 3] = mm(hot_t[...], emb_grad[...]).reshape(32, 2, 16, D).astype(BF16)
+    def give(half):
+        def step(i, carry):
+            first = lax.rem(lax.div(w, 8) + i, 8) * 8
+            rows = pl.ds(pl.multiple_of(first * CAP, 192), 192)
+            cold_send[half, pl.ds(first, 8)] = pack(mm(place_t[rows, :], emb_grad[:, half * HALF : (half + 1) * HALF]))
+            for j in range(8):
+                p = first + j
+
+                @pl.when(p != w)
+                def _():
+                    exchange(2 + half, cold_send.at[half], cold_got.at[half], p).start()
+
+            return carry
+
+        lax.fori_loop(0, 8, step, 0)
+        own = pltpu.make_async_copy(cold_send.at[half, w], cold_got.at[half, w], loc_sem.at[2 + half])
+        own.start()
+        return own
+
+    def sums(half):
+        cols = slice(half * HALF, (half + 1) * HALF)
+
+        def weight_grad(cb, carry):
+            grad = mm_tn(proj_cot[:, pl.ds(pl.multiple_of(cb * D, D), D)], normed[:, cols]).reshape(8, 2, 2, 16, HALF).astype(BF16)
+            for c in range(2):
+                for part in range(2):
+                    wsum[half, c, part, pl.ds(cb * 8, 8)] = grad[:, c, part]
+            return carry
+
+        lax.fori_loop(0, 4, weight_grad, 0)
+        out_grad = mm_tn(masked[...], mixed[:, cols]).reshape(WIDE, 8, HALF)
+        gains = jnp.broadcast_to(gain_sum[:, cols].reshape(1, 1, HALF), (WIDE, 8, HALF))
+        both = jnp.concatenate([out_grad, gains], axis=1).reshape(32, 2, 16, HALF).astype(BF16)
+        hots = mm(hot_t[...], emb_grad[:, cols]).reshape(32, 2, 16, HALF).astype(BF16)
+        for c in range(2):
+            wsum[half, c, 2] = both[:, c]
+            wsum[half, c, 3] = hots[:, c]
 
     peer = w + 1 - 2 * core
-
-    def core_copy(d):
+    order = (2, 1, 3, 0)
+
+    def remote(src, dst, sems, index, to):
+        return pltpu.make_async_remote_copy(
+            src_ref=src, dst_ref=dst, send_sem=sems[0].at[index], recv_sem=sems[1].at[index],
+            device_id=to, device_id_type=MESH,
+        )
+
+    def core_copy(half, d):
         part = lax.rem(n + d, NARROW)
-        return pltpu.make_async_remote_copy(
-            src_ref=wsum.at[:, 1 - core, part], dst_ref=core_got.at[part], send_sem=core_ss.at[d], recv_sem=core_rs.at[d],
-            device_id=(peer, n), device_id_type=MESH,
-        )
-
-    def x_copy(d):
+        return remote(wsum.at[half, 1 - core, part], core_got.at[half, part], (core_ss, core_rs), half * 4 + d, (peer, n))
+
+    def x_copy(half, d):
         part = lax.rem(n + d, NARROW)
-        return pltpu.make_async_remote_copy(
-            src_ref=core_sum.at[part], dst_ref=x_got.at[d - 1], send_sem=x_ss.at[d - 1], recv_sem=x_rs.at[d - 1],
-            device_id=(w, part), device_id_type=MESH,
-        )
-
-    order = (2, 1, 3, 0)
-    for d in order:
-        core_copy(d).start()
-    for d in order:
-        core_copy(d).wait_recv()
-        part = lax.rem(n + d, NARROW)
-        core_sum[part] = (wsum[:, core, part].astype(F32) + core_got[part].astype(F32)).astype(BF16)
-        if d:
-            x_copy(d).start()
-    total = core_sum[n].astype(F32)
-    for d in (1, 3, 2):
-        x_copy(d).wait_recv()
-        total = total + x_got[d - 1].astype(F32)
-    x_sum[...] = total.astype(BF16).reshape(4, 8, 16, D)
-
-    def y_copy(d):
+        return remote(core_sum.at[half, part], x_got.at[half, d - 1], (x_ss, x_rs), half * 3 + d - 1, (w, part))
+
+    def y_copy(half, d):
         to = lax.rem(y + d, 4)
-        return pltpu.make_async_remote_copy(
-            src_ref=x_sum.at[to], dst_ref=y_got.at[d - 1], send_sem=y_ss.at[d - 1], recv_sem=y_rs.at[d - 1],
-            device_id=((to * 8 + z) * 2 + core, n), device_id_type=MESH,
-        )
-
-    def z_copy(d):
+        return remote(
+            x_sum.at[half, to], y_got.at[half, d - 1], (y_ss, y_rs), half * 3 + d - 1, ((to * 8 + z) * 2 + core, n)
+        )
+
+    def z_copy(half, d):
         to = lax.rem(z + d, 8)
-        return pltpu.make_async_remote_copy(
-            src_ref=y_sum.at[to], dst_ref=z_got.at[d - 1], send_sem=z_ss.at[d - 1], recv_sem=z_rs.at[d - 1],
-            device_id=((y * 8 + to) * 2 + core, n), device_id_type=MESH,
-        )
-
-    def g_copy(d):
+        return remote(
+            y_sum.at[half, to], z_got.at[half, d - 1], (z_ss, z_rs), half * 7 + d - 1, ((y * 8 + to) * 2 + core, n)
+        )
+
+    def g_copy(half, d):
         to = lax.rem(n + d, NARROW)
-        return pltpu.make_async_remote_copy(
-            src_ref=gathered.at[n], dst_ref=gathered.at[n], send_sem=g_ss.at[d - 1], recv_sem=g_rs.at[d - 1],
-            device_id=(w, to), device_id_type=MESH,
-        )
-
-    def cx_copy(d):
+        return remote(gathered.at[half, n], gathered.at[half, n], (g_ss, g_rs), half * 3 + d - 1, (w, to))
+
+    def cx_copy(half, d):
         to = lax.rem(n + d, NARROW)
-        return pltpu.make_async_remote_copy(
-            src_ref=cx_send.at[d - 1], dst_ref=cx_got.at[d - 1], send_sem=cx_ss.at[d - 1], recv_sem=cx_rs.at[d - 1],
-            device_id=(w, to), device_id_type=MESH,
-        )
-
-    for d in (2, 1, 3):
-        y_copy(d).start()
-    total = x_sum[y].astype(F32)
-    for d in (1, 3, 2):
-        y_copy(d).wait_recv()
-        total = total + y_got[d - 1].astype(F32)
-    y_sum[...] = total.astype(BF16)
-    for d in range(1, 8):
-        z_copy(d).start()
-    total = y_sum[z].astype(F32)
-    for d in range(1, 8):
-        z_copy(d).wait_recv()
-        total = total + z_got[d - 1].astype(F32)
-    gathered[n] = total
-    for d in range(1, NARROW):
-        g_copy(d).start()
+        return remote(cx_send.at[half, d - 1], cx_got.at[half, d - 1], (cx_ss, cx_rs), half * 3 + d - 1, (w, to))
+
+    def core_start(half):
+        for d in order:
+            core_copy(half, d).start()
+
+    def core_step(half):
+        for d in order:
+            core_copy(half, d).wait_recv()
+            part = lax.rem(n + d, NARROW)
+            core_sum[half, part] = (wsum[half, core, part].astype(F32) + core_got[half, part].astype(F32)).astype(BF16)
+            if d:
+                x_copy(half, d).start()
+
+    def x_step(half):
+        total = core_sum[half, n].astype(F32)
+        for d in (1, 3, 2):
+            x_copy(half, d).wait_recv()
+            total = total + x_got[half, d - 1].astype(F32)
+        x_sum[half] = total.astype(BF16).reshape(4, 8, 16, HALF)
+        for d in (2, 1, 3):
+            y_copy(half, d).start()
+
+    def y_step(half):
+        total = x_sum[half, y].astype(F32)
+        for d in (1, 3, 2):
+            y_copy(half, d).wait_recv()
+            total = total + y_got[half, d - 1].astype(F32)
+        y_sum[half] = total.astype(BF16)
+        for d in range(1, 8):
+            z_copy(half, d).start()
+
+    def z_step(half):
+        total = y_sum[half, z].astype(F32)
+        for d in range(1, 8):
+            z_copy(half, d).wait_recv()
+            total = total + z_got[half, d - 1].astype(F32)
+        gathered[half, n] = total
+        for d in range(1, NARROW):
+            g_copy(half, d).start()
+
+    def cold_step(half, own, line):
+        cols = slice(half * HALF, (half + 1) * HALF)
+        own.wait()
+        await_all(a2a_recv.at[2 + half], cold_got.at[half])
+        unpack_into(rows_in, cold_got.at[half], half * HALF)
+
+        def quarter(part):
+            at = iota((256, WIDE * CAP), 0) + (part * 256).astype(F32)
+            return mm(onehot(at == line), rows_in[:, cols])
+
+        for d in (2, 1, 3):
+            cx_send[half, d - 1] = quarter(lax.rem(n + d, NARROW)).astype(BF16)
+            cx_copy(half, d).start()
+        cold_own[:, cols] = quarter(n)
+
+    own0 = give(0)
+    sums(0)
+    core_start(0)
+    own1 = give(1)
+    core_step(0)
+    sums(1)
+    core_start(1)
+    core_step(1)
 
     asked = want[...].reshape(WIDE, 128)
     high = jnp.floor(asked * (1.0 / 32.0))
@@ -430,54 +488,61 @@
     mine = (line64 >= start) & (line64 < start + CAP)
     asked_line = jnp.sum(jnp.where(mine, spread_out, 0.0), axis=0, keepdims=True)
 
-    own_cold.wait()
-    await_all(a2a_recv.at[2], cold_got)
-    unpack_into(rows_in, cold_got)
-
-    def quarter(part):
-        at = iota((256, WIDE * CAP), 0) + (part * 256).astype(F32)
-        return mm(onehot(at == asked_line), rows_in[...])
-
-    for d in (2, 1, 3):
-        cx_send[d - 1] = quarter(lax.rem(n + d, NARROW)).astype(BF16)
-        cx_copy(d).start()
-    cold_out[...] = quarter(n)
-
-    for d in range(1, NARROW):
-        g_copy(d).wait_recv()
-    proj_out[...] = gathered[0:2].reshape(32, D).T
-    out_out[...] = gathered[2, 0:8].T
-    gain_out[...] = gathered[2, 8:9]
-    for k in range(NARROW):
-
-        @pl.when(n == k)
-        def _():
-            hot_out[...] = gathered[3, 4 * k : 4 * k + 4]
-
-    for d in (1, 3, 2):
-        cx_copy(d).wait_recv()
-        cold_out[...] += cx_got[d - 1].astype(F32)
+    x_step(0)
+    cold_step(0, own0, asked_line)
+    y_step(0)
+    x_step(1)
+    cold_step(1, own1, asked_line)
+    z_step(0)
+    y_step(1)
+    z_step(1)
+    for half in range(2):
+        for d in range(1, NARROW):
+            g_copy(half, d).wait_recv()
+    gathered_out[...] = gathered[...]
+    for half in range(2):
+        for d in range(1, NARROW):
+            cx_copy(half, d).wait_recv()
 
     await_all(a2a_send.at[0], req)
     await_all(a2a_send.at[1], reply)
-    await_all(a2a_send.at[2], cold_send)
-    for d in range(NARROW):
-        core_copy(d).wait_send()
-    for d in range(1, NARROW):
-        x_copy(d).wait_send()
-        y_copy(d).wait_send()
-        g_copy(d).wait_send()
-        cx_copy(d).wait_send()
-    for d in range(1, 8):
-        z_copy(d).wait_send()
+    for half in range(2):
+        await_all(a2a_send.at[2 + half], cold_send.at[half])
+        for d in range(NARROW):
+            core_copy(half, d).wait_send()
+        for d in range(1, NARROW):
+            x_copy(half, d).wait_send()
+            y_copy(half, d).wait_send()
+            g_copy(half, d).wait_send()
+            cx_copy(half, d).wait_send()
+        for d in range(1, 8):
+            z_copy(half, d).wait_send()
+
+
+def finish(gathered, cold_own, cx_got, proj_out, out_out, gain_out, cold_out, hot_out, turned):
+    w = lax.axis_index("wide")
+    n = lax.axis_index("narrow")
+    for half in range(2):
+        cols = slice(half * HALF, (half + 1) * HALF)
+        proj_out[:, cols] = gathered[half, 0:2].reshape(32, HALF)
+        out_out[:, cols] = gathered[half, 2, 0:8]
+        turned[cols, :] = gathered[half, 2, 8:16].T
+        for k in range(NARROW):
+
+            @pl.when(n == k)
+            def _():
+                hot_out[:, cols] = gathered[half, 3, 4 * k : 4 * k + 4]
+
+        total = cold_own[:, cols]
+        for d in range(NARROW - 1):
+            total = total + cx_got[half, d].astype(F32)
+        cold_out[:, cols] = total
+    gain_out[...] = turned[pl.ds(pl.multiple_of(w * 8, 8), 8), :].T[0:1, :]
 
 
 def local(
     item_owner, item_row, hot_row, hot_flag, seq_length, cold_table, hot_table, proj_weight, out_weight, norm_gain, cotangent
 ):
-    hot_id = jnp.where(hot_flag == 1, hot_row, -1)
-    tok = jnp.concatenate([a.reshape(8, 128) for a in (item_owner, item_row, hot_id)], axis=0).astype(F32)
-    tok = jnp.concatenate([tok, jnp.zeros((8, 128), F32)], axis=0)
     vm = pl.BlockSpec(memory_space=pltpu.VMEM)
     sm = pl.BlockSpec(memory_space=pltpu.SMEM)
     v = pltpu.VMEM
@@ -485,33 +550,40 @@
     slots = WIDE * CAP
     block = (WIDE, 48, 256)
     scratch = [
-        v((8, 128), F32), v((WIDE, 1, 128), F32), v((WIDE, 1, 128), F32),
+        v((ROWS, D), BF16), v((TOK, D), BF16), v((D, 4 * D), BF16), v((D, D), BF16), v((TOK, D), BF16),
+        v((32, 128), F32), v((8, 128), F32), v((WIDE, 1, 128), F32), v((WIDE, 1, 128), F32),
         v(block, BF16), v(block, BF16), v((slots, D), BF16), v((slots, TOK), BF16), v((TOK, TOK), BF16),
-        v((TOK, D), BF16), v((TOK, D), BF16), v((TOK, D), F32), v((TOK, 1), F32),
+        v((TOK, D), BF16), v((TOK, D), BF16), v((LEN, D), F32), v((LEN, 1), F32),
         v((LEN, 4 * D), BF16), v((LEN, 4 * D), F32), v((HEADS, LEN, LEN), BF16), v((HEADS, LEN, LEN), F32),
         v((LEN, D), F32), v((TOK, D), BF16), v((TOK, D), BF16), v((TOK, D), BF16), v((LEN, D), BF16),
         v((TOK, 4 * D), BF16), v((TOK, D), BF16), v((1, D), F32),
-        v(block, BF16), v(block, BF16),
-        v((32, 2, 4, 16, D), BF16), v((4, 32, 16, D), BF16), v((4, 32, 16, D), BF16), v((3, 32, 16, D), BF16),
-        v((4, 8, 16, D), BF16), v((3, 8, 16, D), BF16), v((8, 16, D), BF16), v((7, 16, D), BF16), v((4, 16, D), F32),
-        v((3, 256, D), BF16), v((3, 256, D), BF16),
-        dma((3,)), dma((3,)), dma((3,)), dma((4,)), dma((4,)), dma((3,)), dma((3,)), dma((3,)), dma((3,)),
-        dma((7,)), dma((7,)), dma((3,)), dma((3,)), dma((3,)), dma((3,)),
+        v((2, WIDE, 48, 128), BF16), v((2, WIDE, 48, 128), BF16),
+        v((2, 2, 4, 32, 16, HALF), BF16), v((2, 4, 32, 16, HALF), BF16), v((2, 4, 32, 16, HALF), BF16),
+        v((2, 3, 32, 16, HALF), BF16), v((2, 4, 8, 16, HALF), BF16), v((2, 3, 8, 16, HALF), BF16),
+        v((2, 8, 16, HALF), BF16), v((2, 7, 16, HALF), BF16), v((2, 4, 16, HALF), F32), v((2, 3, 256, HALF), BF16),
+        dma((5,)), dma((4,)), dma((4,)), dma((4,)), dma((8,)), dma((8,)), dma((6,)), dma((6,)), dma((6,)), dma((6,)),
+        dma((14,)), dma((14,)), dma((6,)), dma((6,)), dma((6,)), dma((6,)),
     ]
-    out_shape = [
-        jax.ShapeDtypeStruct((D, 32), F32), jax.ShapeDtypeStruct((D, 8), F32), jax.ShapeDtypeStruct((1, D), F32),
-        jax.ShapeDtypeStruct((256, D), F32), jax.ShapeDtypeStruct((4, D), F32),
-    ]
-    proj, out, gain, cold, hot = pl.pallas_call(
+    shape = jax.ShapeDtypeStruct
+    parts = pl.pallas_call(
         kernel,
-        out_shape=out_shape,
-        in_specs=[vm, sm] + [vm] * 6,
-        out_specs=[vm] * 5,
+        out_shape=[shape((2, 4, 16, HALF), F32), shape((256, D), F32), shape((2, 3, 256, HALF), BF16)],
+        in_specs=[vm] * 4 + [sm, vm] + [pl.BlockSpec(memory_space=pl.ANY)] * 5,
+        out_specs=[vm] * 3,
         scratch_shapes=scratch,
         compiler_params=pltpu.CompilerParams(collective_id=0, has_side_effects=True, vmem_limit_bytes=62 * 1024 * 1024),
-    )(tok, seq_length, cold_table, hot_table, proj_weight, out_weight, norm_gain, cotangent.reshape(TOK, D))
-    gain = lax.dynamic_slice(gain, (0, lax.axis_index("wide") * 8), (1, 8))
-    return proj, out, gain, cold, hot
+    )(
+        item_owner.transpose(0, 2, 1), item_row, hot_row, hot_flag, seq_length, norm_gain,
+        cold_table, hot_table, proj_weight, out_weight, cotangent.reshape(TOK, D),
+    )
+    proj, out, gain, cold, hot = pl.pallas_call(
+        finish,
+        out_shape=[shape((32, D), F32), shape((8, D), F32), shape((1, 8), F32), shape((256, D), F32), shape((4, D), F32)],
+        in_specs=[vm] * 3,
+        out_specs=[vm] * 5,
+        scratch_shapes=[v((D, 8), F32)],
+    )(*parts)
+    return proj.T, out.T, gain, cold, hot
 
 
 def solution(mesh):

time: 162 us -> 137 us (0.85)
  Pallas kernels: 151 us -> 136 us
  local copies, waits for them, and re-layouts: 9.03 us -> 0 us
    pallas_call x1 -> x2, Pallas kernels: 151 us -> 136 us  [the longest x1 134 us: local(): pl.pallas_call(kernel, out_shape=[shape((2, 4, 16, HALF), F32), shape((25...]
    unnamed x4 -> x0, local copies, waits for them, and re-layouts: 6.51 us -> none
where the time goes in v2:
time: 137 us
  Pallas kernels  136 us (99%)
    pallas_call x1, Pallas kernels, local(): pl.pallas_call(kernel, out_shape=[shape((2, 4, 16, HALF), F32), shape((25...  134 us

profile of v2, /device:TPU:1, one launch (start us, length us, event | category | flops | bytes accessed | tf_op | source)
XLA Modules:
  0.0 136.7 jit_solution(2917050563714458766)
XLA Ops:
  0.6 133.6 %shard_map.146 = (f32[2,4,16,256]{3,2,1,0:T(8,128)}, f32[256,512]{1,0:T(8,128)}, bf16[2,3,256,256]{3,2,1,0:T(8,128)(2,1)}) custom-call(s32[2,1,512]{2,1,0:T(1,128)} %bitcast.5, s32[2,512]{1,0:T(2,128)} %row_in.1, s32[2,512]{1,0:T(2,128)} %hot_row.1, s32[2,512]{1,0:T(2,128)} %hot_flag.1, s32[2]{0:T(128)} %lens.1, f32[1,512]{1,0:T(1,128)} %gain.1, ...), custom_call_target="tpu_custom_call" | custom-call | tf_op jit(solution)/shard_map/pallas_call | solution.py:568
  134.2 2.5 %shard_map.147 = (f32[32,512]{1,0:T(8,128)}, f32[8,512]{1,0:T(8,128)}, f32[1,8]{1,0:T(1,128)}, f32[256,512]{1,0:T(8,128)}, f32[4,512]{1,0:T(4,128)}) custom-call(f32[2,4,16,256]{3,2,1,0:T(8,128)} %get-tuple-element.13.gathered, f32[256,512]{1,0:T(8,128)} %get-tuple-element.14.cold_own, bf16[2,3,256,256]{3,2,1,0:T(8,128)(2,1)} %get-tuple-element.15.cx_got), custom_call_target="tpu_custom_call" | custom-call | tf_op jit(solution)/shard_map/pallas_call | solution.py:579

commit v3 on v2

v3 whole, which is shorter than its diff:
```python
import functools

import jax
import jax.numpy as jnp
from jax import lax
from jax.experimental import pallas as pl
from jax.experimental.pallas import tpu as pltpu
from jax.sharding import PartitionSpec as P

WIDE = 64
NARROW = 4
CAP = 24
TOK = 1024
LEN = 512
D = 512
HALF = 256
HEADS = 4
ROWS = 1024
EPS = 1e-05
SCALE = 128 ** (-0.5)
MESH = pl.DeviceIdType.MESH
F32 = jnp.float32
BF16 = jnp.bfloat16


def mm(a, b):
    return jnp.dot(a, b, preferred_element_type=F32)


def mm_nt(a, b):
    return lax.dot_general(a, b, (((1,), (1,)), ((), ())), preferred_element_type=F32)


def mm_tn(a, b):
    return lax.dot_general(a, b, (((0,), (0,)), ((), ())), preferred_element_type=F32)


def iota(shape, dim):
    return lax.broadcasted_iota(jnp.int32, shape, dim).astype(F32)


def sigmoid(x):
    return 0.5 * jnp.tanh(0.5 * x) + 0.5


def onehot(mask):
    return jnp.where(mask, 1.0, 0.0).astype(BF16)


def mean(x):
    return jnp.mean(x, axis=-1, keepdims=True)


def pack(rows):
    half = rows.shape[1] // 2
    blocks = rows.reshape(-1, CAP, rows.shape[1])
    return jnp.concatenate([blocks[:, :, :half], blocks[:, :, half:]], axis=1).astype(BF16)


def kernel(
    owner, row_in, hot_row, hot_flag, lens, gain, table_in, hot_table_in, weight_in, out_weight_in, cot_in,
    proj_out, out_out, gain_out, cold_out, hot_out,
    table, hot_table, weight, out_weight, cot, tok, slots, req, want, reply, got, rows_in, place_t, hot_t, emb, normed, xhat, spread, acted, dact,
    attn, dattn, per_head, mixed, masked, mixed_cot, dhead, proj_cot, emb_grad, gain_sum,
    cold_send, cold_got, wsum, core_got, core_sum, x_got, x_on, x_on_got, x_sum, y_got, y_sum, z_got, gathered, cx_send, cx_got, quarter_t, turned,
    load_sem, loc_sem, a2a_send, req_recv, rep_recv, cold_recv, core_ss, core_rs, x_ss, x_rs, y_ss, y_rs, z_ss, z_rs, g_ss, g_rs, cx_ss, cx_rs,
):
    w = lax.axis_index("wide")
    n = lax.axis_index("narrow")
    core = lax.rem(w, 2)
    chip = lax.div(w, 2)
    z = lax.rem(chip, 8)
    y = lax.div(chip, 8)

    loads = [
        pltpu.make_async_copy(src, dst, load_sem.at[i])
        for i, (src, dst) in enumerate(
            [(table_in, table), (hot_table_in, hot_table), (cot_in, cot), (out_weight_in, out_weight), (weight_in, weight)]
        )
    ]
    for load in loads:
        load.start()

    barrier = pltpu.get_barrier_semaphore()

    def greet(d, carry):
        pl.semaphore_signal(barrier, inc=1, device_id=(lax.rem(w + d, WIDE), n), device_id_type=MESH)
        return carry

    lax.fori_loop(1, WIDE, greet, 0)
    for d in range(1, NARROW):
        pl.semaphore_signal(barrier, inc=1, device_id=(w, lax.rem(n + d, NARROW)), device_id_type=MESH)

    for a in range(8):
        at = (slice(a // 4, a // 4 + 1), slice(a % 4 * 128, a % 4 * 128 + 128))
        tok[a : a + 1, :] = owner[a // 4, :, at[1]].astype(F32)
        tok[8 + a : 9 + a, :] = row_in[at].astype(F32)
        tok[16 + a : 17 + a, :] = jnp.where(hot_flag[at] == 1, hot_row[at], -1).astype(F32)

    upper = onehot(iota((128, 128), 0) < iota((128, 128), 1))
    sub = iota((128, 128), 0)
    carry = jnp.zeros((128, 1), F32)
    req_hi = jnp.zeros((128, 128), F32)
    req_lo = jnp.zeros((128, 128), F32)
    for a in range(8):
        own = tok[a : a + 1, :]
        row = tok[8 + a : 9 + a, :]
        hot = tok[16 + a : 17 + a, :]
        owns = jnp.where(sub == own, 1.0, 0.0)
        owns_b = owns.astype(BF16)
        before = mm(owns_b, upper) + carry
        rank = jnp.sum(owns * before, axis=0, keepdims=True)
        carry = carry + jnp.sum(owns, axis=1, keepdims=True)
        slots[a : a + 1, :] = jnp.where(hot >= 0.0, -1.0, own * CAP + rank)
        high = jnp.floor(row * (1.0 / 32.0))
        low = row - 32.0 * high
        ranked = sub == rank
        req_hi = req_hi + mm_nt(owns_b, jnp.where(ranked, high, 0.0).astype(BF16))
        req_lo = req_lo + mm_nt(owns_b, jnp.where(ranked, low, 0.0).astype(BF16))
    asked = 32.0 * req_hi + req_lo
    for o in range(WIDE):
        req[o] = asked[o : o + 1, :]

    pl.semaphore_wait(barrier, WIDE - 1 + NARROW - 1)

    group = lax.div(w, 8)

    def exchange(src, dst, sends, recv, p):
        return pltpu.make_async_remote_copy(
            src_ref=src, dst_ref=dst, send_sem=a2a_send.at[sends], recv_sem=recv, device_id=(p, n), device_id_type=MESH
        )

    def await_bytes(sem, view):
        pltpu.make_async_copy(view, view, sem).wait()

    others = pl.ds(0, WIDE - 1)

    def ask(d, carry):
        p = lax.rem(w + d, WIDE)
        exchange(req.at[p], want.at[w], 0, req_recv.at[group], p).start()
        return carry

    lax.fori_loop(1, WIDE, ask, 0)
    pltpu.make_async_copy(req.at[w], want.at[w], req_recv.at[group]).start()
    loads[0].wait()

    lanes = iota((CAP, ROWS), 1)

    def answer(i, carry):
        which = lax.rem(group + i, 8)
        first = which * 8
        eight = pl.ds(first, 8)
        await_bytes(req_recv.at[which], want.at[eight])
        asked8 = want[eight].reshape(8, 128).T
        picks = jnp.concatenate([jnp.where(lanes == asked8[:CAP, j : j + 1], 1.0, 0.0) for j in range(8)], axis=0)
        reply[eight] = pack(mm(picks.astype(BF16), table[...]))
        for j in range(8):
            p = first + j

            @pl.when(p != w)
            def _():
                exchange(reply.at[p], got.at[w], 1, rep_recv.at[group], p).start()

        return carry

    lax.fori_loop(0, 8, answer, 0)
    pltpu.make_async_copy(reply.at[w], got.at[w], rep_recv.at[group]).start()

    def build_place(a, carry):
        rows = pl.ds(pl.multiple_of(a * 192, 192), 192)
        at = iota((192, 128), 0) + (a * 192).astype(F32)
        for b in range(8):
            place_t[rows, b * 128 : (b + 1) * 128] = onehot(at == slots[b : b + 1, :])
        return carry

    lax.fori_loop(0, 8, build_place, 0)

    def build_hot(a, carry):
        rows = pl.ds(pl.multiple_of(a * 128, 128), 128)
        at = iota((128, 128), 0) + (a * 128).astype(F32)
        for b in range(8):
            hot_t[rows, b * 128 : (b + 1) * 128] = onehot(at == tok[16 + b : 17 + b, :])
        return carry

    lax.fori_loop(0, 8, build_hot, 0)
    for load in loads[1:]:
        load.wait()
    tok_cols = tok[...].T
    for half in range(2):
        rows = slice(half * LEN, (half + 1) * LEN)
        hots = jnp.concatenate(
            [onehot(iota((128, TOK), 1) == tok_cols[:, 16 + a : 17 + a]) for a in range(half * 4, half * 4 + 4)], axis=0
        )
        emb[rows, :] = mm(hots, hot_table[...]).astype(BF16)
        live = iota((LEN, 1), 0) < lens[half].astype(F32)
        masked[rows, :] = jnp.where(live, cot[rows, :].astype(F32), 0.0).astype(BF16)
        mixed_cot[rows, :] = mm_nt(masked[rows, :], out_weight[...]).astype(BF16)

    slot_cols = slots[...].T

    def place(i, carry):
        which = lax.rem(group - i + 8, 8)
        eight = pl.ds(which * 8, 8)
        await_bytes(rep_recv.at[which], got.at[eight])
        block = got[eight].astype(F32)
        rows_8 = jnp.concatenate([block[:, :CAP].reshape(192, HALF), block[:, CAP:].reshape(192, HALF)], axis=1)
        at = iota((128, 192), 1) + (which * 192).astype(F32)
        picks = jnp.concatenate([onehot(at == slot_cols[:, a : a + 1]) for a in range(8)], axis=0)
        emb[...] = (emb[...].astype(F32) + mm(picks, rows_8.astype(BF16))).astype(BF16)
        return carry

    lax.fori_loop(0, 8, place, 0)

    gain_sum[...] = jnp.zeros_like(gain_sum)

    def layer(s, carry):
        base = s * LEN
        rows = pl.ds(pl.multiple_of(base, LEN), LEN)
        length = lens[s].astype(F32)

        def norm(t, c):
            part = pl.ds(pl.multiple_of(base + t * 256, 256), 256)
            here = pl.ds(pl.multiple_of(t * 256, 256), 256)
            x = emb[part, :].astype(F32)
            center = x - mean(x)
            r = lax.rsqrt(mean(center * center) + EPS)
            hat = center * r
            xhat[here, :] = hat
            spread[here, :] = r
            normed[part, :] = (hat * gain[...]).astype(BF16)
            return c

        lax.fori_loop(0, 2, norm, 0)

        def project(cb, c):
            def raw(i):
                return mm(normed[rows, :], weight[:, i * 256 : i * 256 + 256])

            ahead = raw(0)
            for i in range(8):
                x = 0.5 * ahead
                if i < 7:
                    ahead = raw(i + 1)
                cols = slice(i * 256, i * 256 + 256)
                t = jnp.tanh(x)
                xt = x * t
                acted[:, cols] = (xt + x).astype(BF16)
                dact[:, cols] = ((0.5 * t + 0.5) * (1.0 + x - xt)).astype(BF16)
            return c

        lax.fori_loop(0, 1, project, 0)

        def cols_of(block, h):
            return pl.ds(pl.multiple_of(block * D + h * 128, 128), 128)

        inverse = jnp.where(iota((1, LEN), 1) < length, 1.0 / jnp.full((1, LEN), length), 0.0)

        def attend(pair, c):
            for h in [pair * 4 + i for i in range(4)]:
                for part in range(2):
                    keys = 256 * (part + 1)
                    at = slice(256 * part, 256 * part + 256)
                    k = acted[:keys, cols_of(3, h)]
                    x = mm_nt(acted[at, cols_of(2, h)], k) * (0.5 * SCALE)
                    t = jnp.tanh(x)
                    xt = x * t
                    a = xt + x
                    slope = (t + 1.0) * (1.0 + x - xt)
                    weights = []
                    for block in range(part + 1):
                        these = slice(256 * block, 256 * block + 256)
                        scale = inverse[:, these]
                        if block == part:
                            scale = jnp.where(iota((256, 256), 1) <= iota((256, 256), 0), scale, 0.0)
                        weights.append((a[:, these] * scale).astype(BF16))
                        attn[h, at, these] = weights[-1]
                        dattn[h, at, these] = (slope[:, these] * scale).astype(BF16)
                    w_all = weights[0] if part == 0 else jnp.concatenate(weights, axis=1)
                    per_head[at, pl.ds(pl.multiple_of(h * 128, 128), 128)] = mm(w_all, acted[:keys, cols_of(1, h)])
            return c

        lax.fori_loop(0, 1, attend, 0)

        def gate_step(t, c):
            part = pl.ds(pl.multiple_of(t * 256, 256), 256)
            whole = pl.ds(pl.multiple_of(base + t * 256, 256), 256)
            x = per_head[part, :]
            center = x - mean(x)
            r = lax.rsqrt(mean(center * center) + EPS)
            hat = center * r
            gate = acted[part, :D].astype(F32)
            g = mixed_cot[whole, :].astype(F32)
            mixed[whole, :] = (hat * gate).astype(BF16)
            dgate = (g * hat).astype(BF16)
            proj_cot[whole, :D] = dgate * dact[part, :D]
            dhat = g * gate
            dhead[part, :] = (r * (dhat - mean(dhat) - hat * mean(dhat * hat))).astype(BF16)
            return c

        lax.fori_loop(0, 2, gate_step, 0)

        def attend_back(pair, c):
            for h in [pair * 4 + i for i in range(4)]:
                head_back(h)
            return c

        def head_back(h):
            def put(block, at, to, grad):
                cols = cols_of(block, h)
                proj_cot[to, cols] = grad.astype(BF16) * dact[at, cols]

            dks, dvs = [], []
            for part in range(2):
                keys = 256 * (part + 1)
                at = slice(256 * part, 256 * part + 256)
                q = acted[at, cols_of(2, h)]
                k = acted[:keys, cols_of(3, h)]
                v = acted[:keys, cols_of(1, h)]
                do = dhead[at, pl.ds(pl.multiple_of(h * 128, 128), 128)]
                ds = mm_nt(do, v).astype(BF16) * dattn[h, at, :keys]
                put(2, at, pl.ds(pl.multiple_of(base + 256 * part, 256), 256), mm(ds, k) * (0.5 * SCALE))
                dks.append(mm_tn(ds, q) * (0.5 * SCALE))
                dvs.append(mm_tn(attn[h, at, :keys], do))
            for block, grads in ((3, dks), (1, dvs)):
                put(block, slice(0, 256), pl.ds(pl.multiple_of(base, 256), 256), grads[0] + grads[1][:256])
                put(block, slice(256, 512), pl.ds(pl.multiple_of(base + 256, 256), 256), grads[1][256:])

        lax.fori_loop(0, 1, attend_back, 0)

        ncot = mm_nt(proj_cot[rows, :], weight[...])
        hat = xhat[...]
        gain_sum[...] += jnp.sum(ncot * hat, axis=0, keepdims=True)
        d = ncot * gain[...]
        ecot = spread[...] * (d - mean(d) - hat * mean(d * hat))
        total = masked[rows, :].astype(F32) + ecot
        emb_grad[rows, :] = jnp.where(iota((LEN, 1), 0) < length, total, 0.0).astype(BF16)
        return carry

    lax.fori_loop(0, 2, layer, 0)

    def give(half):
        def step(i, carry):
            first = lax.rem(group + i, 8) * 8
            rows = pl.ds(pl.multiple_of(first * CAP, 192), 192)
            cold_send[half, pl.ds(first, 8)] = pack(mm(place_t[rows, :], emb_grad[:, half * HALF : (half + 1) * HALF]))
            for j in range(8):
                p = first + j

                @pl.when(p != w)
                def _():
                    give_copy(half, p).start()

            return carry

        lax.fori_loop(0, 8, step, 0)
        own = pltpu.make_async_copy(cold_send.at[half, w], cold_got.at[half, w], loc_sem.at[half])
        own.start()
        return own

    def message(ref, which, block):
        if which == 0:
            return ref.at[0, block]
        return ref.at[1, block, pl.ds(0, 32)] if which == 1 else ref.at[1, block, pl.ds(32, 16)]

    def give_copy(which, p):
        return exchange(message(cold_send, which, p), message(cold_got, which, w), 2 + which, cold_recv.at[which], p)

    def give_rest(d, carry):
        give_copy(2, lax.rem(w + d, WIDE)).start()
        return carry

    def sums(half):
        cols = slice(half * HALF, (half + 1) * HALF)

        def weight_grad(cb, carry):
            grad = mm_tn(proj_cot[:, pl.ds(pl.multiple_of(cb * D, D), D)], normed[:, cols]).reshape(8, 2, 2, 16, HALF).astype(BF16)
            for c in range(2):
                for part in range(2):
                    wsum[half, c, part, pl.ds(cb * 8, 8)] = grad[:, c, part]
            return carry

        lax.fori_loop(0, 4, weight_grad, 0)
        out_grad = mm_tn(masked[...], mixed[:, cols]).reshape(WIDE, 8, HALF)
        gains = jnp.broadcast_to(gain_sum[:, cols].reshape(1, 1, HALF), (WIDE, 8, HALF))
        both = jnp.concatenate([out_grad, gains], axis=1).reshape(32, 2, 16, HALF).astype(BF16)
        hots = mm(hot_t[...], emb_grad[:, cols]).reshape(32, 2, 16, HALF).astype(BF16)
        for c in range(2):
            wsum[half, c, 2] = both[:, c]
            wsum[half, c, 3] = hots[:, c]

    peer = w + 1 - 2 * core
    sides = (n + 1 - 2 * lax.rem(n, 2), NARROW - 1 - n)
    parts = (lax.rem(n + 2, NARROW), sides[0], sides[1], n)

    def remote(src, dst, sems, index, to):
        return pltpu.make_async_remote_copy(
            src_ref=src, dst_ref=dst, send_sem=sems[0].at[index], recv_sem=sems[1].at[index],
            device_id=to, device_id_type=MESH,
        )

    def core_copy(half, j):
        src = wsum.at[half, 1 - core, parts[j]]
        return remote(src, core_got.at[half, parts[j]], (core_ss, core_rs), half * 4 + j, (peer, n))

    def chips(side):
        return pl.ds(16 * side, 16)

    def x_copy(half, side, on):
        src = core_sum.at[half, parts[0] if on else sides[side], chips(side)]
        return remote(src, x_got.at[half, side, on], (x_ss, x_rs), half * 6 + side * 3 + on, (w, sides[side]))

    def x_on_copy(half, side):
        dst = x_on_got.at[half, side]
        return remote(x_on.at[half, side], dst, (x_ss, x_rs), half * 6 + side * 3 + 2, (w, sides[1 - side]))

    def y_copy(half, d):
        to = lax.rem(y + d, 4)
        return remote(
            x_sum.at[half, to], y_got.at[half, d - 1], (y_ss, y_rs), half * 3 + d - 1, ((to * 8 + z) * 2 + core, n)
        )

    def z_copy(half, d):
        to = lax.rem(z + d, 8)
        return remote(
            y_sum.at[half, to], z_got.at[half, d - 1], (z_ss, z_rs), half * 7 + d - 1, ((y * 8 + to) * 2 + core, n)
        )

    def g_copy(half, d):
        to = lax.rem(n + d, NARROW)
        return remote(gathered.at[half, n], gathered.at[half, n], (g_ss, g_rs), half * 3 + d - 1, (w, to))

    def cx_copy(piece, d):
        to = lax.rem(n + d, NARROW)
        units = pl.ds(0, 2) if piece == 0 else pl.ds(piece + 1, 1)
        return remote(cx_send.at[units, d - 1], cx_got.at[units, d - 1], (cx_ss, cx_rs), piece * 3 + d - 1, (w, to))

    def core_start(half):
        for j in range(4):
            core_copy(half, j).start()

    def core_step(half):
        for j in range(4):
            core_copy(half, j).wait_recv()
            part = parts[j]
            core_sum[half, part] = (wsum[half, core, part].astype(F32) + core_got[half, part].astype(F32)).astype(BF16)
            if j == 0:
                x_copy(half, 0, 1).start()
                x_copy(half, 1, 1).start()
            elif j < 3:
                x_copy(half, j - 1, 0).start()

    def x_pass(half):
        for side in range(2):
            x_copy(half, side, 1).wait_recv()
            mine = core_sum[half, sides[1 - side], chips(side)].astype(F32)
            x_on[half, side] = (mine + x_got[half, side, 1].astype(F32)).astype(BF16)
            x_on_copy(half, side).start()

    def x_step(half):
        for side in range(2):
            x_copy(half, side, 0).wait_recv()
            x_on_copy(half, side).wait_recv()
            total = core_sum[half, n, chips(side)].astype(F32) + x_got[half, side, 0].astype(F32)
            total = total + x_on_got[half, side].astype(F32)
            x_sum[half, 2 * side : 2 * side + 2] = total.astype(BF16).reshape(2, 8, 16, HALF)
        for d in (2, 1, 3):
            y_copy(half, d).start()

    def y_step(half):
        total = x_sum[half, y].astype(F32)
        for d in (1, 3, 2):
            y_copy(half, d).wait_recv()
            total = total + y_got[half, d - 1].astype(F32)
        y_sum[half] = total.astype(BF16)
        for d in range(1, 8):
            z_copy(half, d).start()

    def z_step(half):
        total = y_sum[half, z].astype(F32)
        for d in range(1, 8):
            z_copy(half, d).wait_recv()
            total = total + z_got[half, d - 1].astype(F32)
        gathered[half, n] = total
        for d in range(1, NARROW):
            g_copy(half, d).start()

    def cold_step(piece):
        await_bytes(cold_recv.at[piece], message(cold_got, piece, others))
        units = (0, 1) if piece == 0 else (piece + 1,)

        def unpack(i, carry):
            rows = pl.ds(pl.multiple_of(i * 192, 192), 192)
            for u in units:
                low = 16 * (u % 2)
                block = cold_got[u // 2, pl.ds(i * 8, 8), low : low + 32].astype(F32)
                part = block[:, low // 2 : low // 2 + CAP].reshape(192, 128)
                rows_in[rows, u * 128 : (u + 1) * 128] = part.astype(BF16)
            return carry

        lax.fori_loop(0, 8, unpack, 0)
        cols = slice(units[0] * 128, units[-1] * 128 + 128)

        def quarter(part):
            return mm(quarter_t[part], rows_in[:, cols])

        for d in (2, 1, 3):
            sums_out = quarter(lax.rem(n + d, NARROW)).astype(BF16)
            for i, u in enumerate(units):
                cx_send[u, d - 1] = sums_out[:, i * 128 : (i + 1) * 128]
            cx_copy(piece, d).start()
        cold_out[:, cols] = quarter(n)

    own0 = give(0)
    sums(0)
    core_start(0)
    own1 = give(1)
    lax.fori_loop(1, WIDE, give_rest, 0)
    core_step(0)
    sums(1)
    core_start(1)
    core_step(1)
    x_pass(0)

    asked = want[...].reshape(WIDE, 128)
    high = jnp.floor(asked * (1.0 / 32.0))
    low = asked - 32.0 * high
    line = iota((128, WIDE * CAP), 1)
    within = line - CAP * jnp.floor((line + 0.5) * (1.0 / CAP))
    spot = onehot(within == iota((128, WIDE * CAP), 0))
    spread_out = 32.0 * mm(high.astype(BF16), spot) + mm(low.astype(BF16), spot)
    line64 = iota((WIDE, WIDE * CAP), 1)
    start = iota((WIDE, WIDE * CAP), 0) * CAP
    mine = (line64 >= start) & (line64 < start + CAP)
    asked_line = jnp.sum(jnp.where(mine, spread_out, 0.0), axis=0, keepdims=True)
    for part in range(4):
        quarter_t[part] = onehot(iota((256, WIDE * CAP), 0) + 256.0 * part == asked_line)
    own0.wait()
    own1.wait()

    x_step(0)
    x_pass(1)
    cold_step(0)
    y_step(0)
    x_step(1)
    z_step(0)
    cold_step(1)
    y_step(1)
    cold_step(2)
    z_step(1)
    for half in range(2):
        cols = slice(half * HALF, (half + 1) * HALF)
        for d in range(1, NARROW):
            g_copy(half, d).wait_recv()
        proj_out[:, cols] = gathered[half, 0:2].reshape(32, HALF)
        out_out[:, cols] = gathered[half, 2, 0:8]
        turned[cols, :] = gathered[half, 2, 8:16].T
        for k in range(NARROW):

            @pl.when(n == k)
            def _():
                hot_out[:, cols] = gathered[half, 3, 4 * k : 4 * k + 4]

    gain_out[...] = turned[pl.ds(pl.multiple_of(w * 8, 8), 8), :].T[0:1, :]
    for piece in range(3):
        for d in range(1, NARROW):
            cx_copy(piece, d).wait_recv()
    for u in range(4):
        total = cold_out[:, u * 128 : (u + 1) * 128]
        for d in range(NARROW - 1):
            total = total + cx_got[u, d].astype(F32)
        cold_out[:, u * 128 : (u + 1) * 128] = total

    await_bytes(a2a_send.at[0], req.at[others])
    await_bytes(a2a_send.at[1], reply.at[others])
    for piece in range(3):
        await_bytes(a2a_send.at[2 + piece], message(cold_send, piece, others))
        for d in range(1, NARROW):
            cx_copy(piece, d).wait_send()
    for half in range(2):
        for j in range(4):
            core_copy(half, j).wait_send()
        for side in range(2):
            x_copy(half, side, 0).wait_send()
            x_copy(half, side, 1).wait_send()
            x_on_copy(half, side).wait_send()
        for d in range(1, NARROW):
            y_copy(half, d).wait_send()
            g_copy(half, d).wait_send()
        for d in range(1, 8):
            z_copy(half, d).wait_send()


def finish(*refs):
    sems = refs[-1]
    copies = [pltpu.make_async_copy(refs[i], refs[5 + i], sems.at[i]) for i in range(5)]
    for copy in copies:
        copy.start()
    for copy in copies:
        copy.wait()


def local(
    item_owner, item_row, hot_row, hot_flag, seq_length, cold_table, hot_table, proj_weight, out_weight, norm_gain, cotangent
):
    vm = pl.BlockSpec(memory_space=pltpu.VMEM)
    sm = pl.BlockSpec(memory_space=pltpu.SMEM)
    v = pltpu.VMEM
    dma = pltpu.SemaphoreType.DMA
    slots = WIDE * CAP
    block = (WIDE, 48, 256)
    scratch = [
        v((ROWS, D), BF16), v((TOK, D), BF16), v((D, 4 * D), BF16), v((D, D), BF16), v((TOK, D), BF16),
        v((32, 128), F32), v((8, 128), F32), v((WIDE, 1, 128), F32), v((WIDE, 1, 128), F32),
        v(block, BF16), v(block, BF16), v((slots, D), BF16), v((slots, TOK), BF16), v((TOK, TOK), BF16),
        v((TOK, D), BF16), v((TOK, D), BF16), v((LEN, D), F32), v((LEN, 1), F32),
        v((LEN, 4 * D), BF16), v((LEN, 4 * D), BF16), v((HEADS, LEN, LEN), BF16), v((HEADS, LEN, LEN), BF16),
        v((LEN, D), F32), v((TOK, D), BF16), v((TOK, D), BF16), v((TOK, D), BF16), v((LEN, D), BF16),
        v((TOK, 4 * D), BF16), v((TOK, D), BF16), v((1, D), F32),
        v((2, WIDE, 48, 128), BF16), v((2, WIDE, 48, 128), BF16),
        v((2, 2, 4, 32, 16, HALF), BF16), v((2, 4, 32, 16, HALF), BF16), v((2, 4, 32, 16, HALF), BF16),
        v((2, 2, 2, 16, 16, HALF), BF16), v((2, 2, 16, 16, HALF), BF16), v((2, 2, 16, 16, HALF), BF16),
        v((2, 4, 8, 16, HALF), BF16), v((2, 3, 8, 16, HALF), BF16),
        v((2, 8, 16, HALF), BF16), v((2, 7, 16, HALF), BF16), v((2, 4, 16, HALF), F32),
        v((4, 3, 256, 128), BF16), v((4, 3, 256, 128), BF16), v((4, 256, slots), BF16), v((D, 8), F32),
        dma((5,)), dma((2,)), dma((5,)), dma((8,)), dma((8,)), dma((3,)), dma((8,)), dma((8,)), dma((12,)), dma((12,)), dma((6,)), dma((6,)),
        dma((14,)), dma((14,)), dma((6,)), dma((6,)), dma((9,)), dma((9,)),
    ]
    shape = jax.ShapeDtypeStruct
    results = [shape((32, D), F32), shape((8, D), F32), shape((1, 8), F32), shape((256, D), F32), shape((4, D), F32)]
    hbm = pl.BlockSpec(memory_space=pl.ANY)
    parts = pl.pallas_call(
        kernel,
        out_shape=results,
        in_specs=[vm] * 4 + [sm, vm] + [hbm] * 5,
        out_specs=[vm] * 5,
        scratch_shapes=scratch,
        compiler_params=pltpu.CompilerParams(collective_id=0, has_side_effects=True, vmem_limit_bytes=62 * 1024 * 1024),
    )(
        item_owner.transpose(0, 2, 1), item_row, hot_row, hot_flag, seq_length, norm_gain,
        cold_table, hot_table, proj_weight, out_weight, cotangent.reshape(TOK, D),
    )
    proj, out, gain, cold, hot = pl.pallas_call(
        finish,
        out_shape=results,
        in_specs=[vm] * 5,
        out_specs=[hbm] * 5,
        scratch_shapes=[dma((5,))],
    )(*parts)
    return proj.T, out.T, gain, cold, hot


def solution(mesh):
    both = P(("wide", "narrow"))
    in_specs = (both, both, both, both, both, P("wide"), P(), P(), P(), P(), both)
    out_specs = (P(None, "wide"), P(None, "wide"), P(None, "wide"), both, both)
    return jax.shard_map(local, mesh=mesh, in_specs=in_specs, out_specs=out_specs, check_vma=False)
```

time: 137 us -> 129 us (0.942); the launches traced: 137 us -> 127 us
  Pallas kernels: 136 us -> 126 us
    pallas_call x2, Pallas kernels: 136 us -> 126 us  [the longest x1 124 us: local(): pl.pallas_call(kernel, out_shape=results, in_specs=[vm] * 4 + [sm, vm] +...]
where the time goes in v3:
time: 129 us; the launch traced here: 127 us
  Pallas kernels  126 us (98%)
    pallas_call x1, Pallas kernels, local(): pl.pallas_call(kernel, out_shape=results, in_specs=[vm] * 4 + [sm, vm] +...  124 us

profile of v3, /device:TPU:1, one launch (start us, length us, event | category | flops | bytes accessed | tf_op | source)
XLA Modules:
  0.0 127.1 jit_solution(10225538224729274127)
XLA Ops:
  0.6 124.4 %shard_map.146 = (f32[32,512]{1,0:T(8,128)}, f32[8,512]{1,0:T(8,128)}, f32[1,8]{1,0:T(1,128)}, f32[256,512]{1,0:T(8,128)}, f32[4,512]{1,0:T(4,128)}) custom-call(s32[2,1,512]{2,1,0:T(1,128)} %bitcast.5, s32[2,512]{1,0:T(2,128)} %row_in.1, s32[2,512]{1,0:T(2,128)} %hot_row.1, s32[2,512]{1,0:T(2,128)} %hot_flag.1, s32[2]{0:T(128)} %lens.1, f32[1,512]{1,0:T(1,128)} %gain.1, ...), custom_call_target="tpu_custom_call" | custom-call | tf_op jit(solution)/shard_map/pallas_call | solution.py:631
  125.0 1.9 %shard_map.147 = (f32[32,512]{1,0:T(8,128)}, f32[8,512]{1,0:T(8,128)}, f32[1,8]{1,0:T(1,128)}, f32[256,512]{1,0:T(8,128)}, f32[4,512]{1,0:T(4,128)}) custom-call(f32[32,512]{1,0:T(8,128)} %get-tuple-element.15.refs_0_, f32[8,512]{1,0:T(8,128)} %get-tuple-element.16.refs_1_, f32[1,8]{1,0:T(1,128)} %get-tuple-element.17.refs_2_, ...), custom_call_target="tpu_custom_call" | custom-call | tf_op jit(solution)/shard_map/pallas_call | solution.py:642

commit v4 on v3

--- a/solution.py
+++ b/solution.py
@@ -58,9 +58,9 @@
 
 
 def kernel(
-    owner, row_in, hot_row, hot_flag, lens, gain, table_in, hot_table_in, weight_in, out_weight_in, cot_in,
+    owner_in, row_in_in, hot_row_in, hot_flag_in, lens_in, gain_in, table_in, hot_table_in, weight_in, out_weight_in, cot_in,
     proj_out, out_out, gain_out, cold_out, hot_out,
-    table, hot_table, weight, out_weight, cot, tok, slots, req, want, reply, got, rows_in, place_t, hot_t, emb, normed, xhat, spread, acted, dact,
+    owner, row_in, hot_row, hot_flag, lens, gain, table, hot_table, weight, out_weight, cot, tok, slots, req, want, reply, got, rows_in, place_t, hot_t, emb, normed, xhat, spread, acted, dact,
     attn, dattn, per_head, mixed, masked, mixed_cot, dhead, proj_cot, emb_grad, gain_sum,
     cold_send, cold_got, wsum, core_got, core_sum, x_got, x_on, x_on_got, x_sum, y_got, y_sum, z_got, gathered, cx_send, cx_got, quarter_t, turned,
     load_sem, loc_sem, a2a_send, req_recv, rep_recv, cold_recv, core_ss, core_rs, x_ss, x_rs, y_ss, y_rs, z_ss, z_rs, g_ss, g_rs, cx_ss, cx_rs,
@@ -75,7 +75,11 @@
     loads = [
         pltpu.make_async_copy(src, dst, load_sem.at[i])
         for i, (src, dst) in enumerate(
-            [(table_in, table), (hot_table_in, hot_table), (cot_in, cot), (out_weight_in, out_weight), (weight_in, weight)]
+            [
+                (owner_in, owner), (row_in_in, row_in), (hot_row_in, hot_row), (hot_flag_in, hot_flag), (table_in, table),
+                (lens_in, lens), (gain_in, gain), (hot_table_in, hot_table), (cot_in, cot), (out_weight_in, out_weight),
+                (weight_in, weight),
+            ]
         )
     ]
     for load in loads:
@@ -91,6 +95,8 @@
     for d in range(1, NARROW):
         pl.semaphore_signal(barrier, inc=1, device_id=(w, lax.rem(n + d, NARROW)), device_id_type=MESH)
 
+    for load in loads[:4]:
+        load.wait()
     for a in range(8):
         at = (slice(a // 4, a // 4 + 1), slice(a % 4 * 128, a % 4 * 128 + 128))
         tok[a : a + 1, :] = owner[a // 4, :, at[1]].astype(F32)
@@ -142,7 +148,7 @@
 
     lax.fori_loop(1, WIDE, ask, 0)
     pltpu.make_async_copy(req.at[w], want.at[w], req_recv.at[group]).start()
-    loads[0].wait()
+    loads[4].wait()
 
     lanes = iota((CAP, ROWS), 1)
 
@@ -183,7 +189,7 @@
         return carry
 
     lax.fori_loop(0, 8, build_hot, 0)
-    for load in loads[1:]:
+    for load in loads[5:]:
         load.wait()
     tok_cols = tok[...].T
     for half in range(2):
@@ -327,13 +333,16 @@
 
         lax.fori_loop(0, 1, attend_back, 0)
 
-        ncot = mm_nt(proj_cot[rows, :], weight[...])
-        hat = xhat[...]
-        gain_sum[...] += jnp.sum(ncot * hat, axis=0, keepdims=True)
-        d = ncot * gain[...]
-        ecot = spread[...] * (d - mean(d) - hat * mean(d * hat))
-        total = masked[rows, :].astype(F32) + ecot
-        emb_grad[rows, :] = jnp.where(iota((LEN, 1), 0) < length, total, 0.0).astype(BF16)
+        for t in range(2):
+            here = slice(256 * t, 256 * t + 256)
+            part = pl.ds(pl.multiple_of(base + 256 * t, 256), 256)
+            ncot = mm_nt(proj_cot[part, :], weight[...])
+            hat = xhat[here, :]
+            gain_sum[...] += jnp.sum(ncot * hat, axis=0, keepdims=True)
+            d = ncot * gain[...]
+            ecot = spread[here, :] * (d - mean(d) - hat * mean(d * hat))
+            total = masked[part, :].astype(F32) + ecot
+            emb_grad[part, :] = jnp.where(iota((256, 1), 0) + 256.0 * t < length, total, 0.0).astype(BF16)
         return carry
 
     lax.fori_loop(0, 2, layer, 0)
@@ -369,17 +378,8 @@
         give_copy(2, lax.rem(w + d, WIDE)).start()
         return carry
 
-    def sums(half):
+    def sums_a(half):
         cols = slice(half * HALF, (half + 1) * HALF)
-
-        def weight_grad(cb, carry):
-            grad = mm_tn(proj_cot[:, pl.ds(pl.multiple_of(cb * D, D), D)], normed[:, cols]).reshape(8, 2, 2, 16, HALF).astype(BF16)
-            for c in range(2):
-                for part in range(2):
-                    wsum[half, c, part, pl.ds(cb * 8, 8)] = grad[:, c, part]
-            return carry
-
-        lax.fori_loop(0, 4, weight_grad, 0)
         out_grad = mm_tn(masked[...], mixed[:, cols]).reshape(WIDE, 8, HALF)
         gains = jnp.broadcast_to(gain_sum[:, cols].reshape(1, 1, HALF), (WIDE, 8, HALF))
         both = jnp.concatenate([out_grad, gains], axis=1).reshape(32, 2, 16, HALF).astype(BF16)
@@ -388,6 +388,18 @@
             wsum[half, c, 2] = both[:, c]
             wsum[half, c, 3] = hots[:, c]
 
+    def sums_b(half):
+        cols = slice(half * HALF, (half + 1) * HALF)
+
+        def weight_grad(cb, carry):
+            grad = mm_tn(proj_cot[:, pl.ds(pl.multiple_of(cb * D, D), D)], normed[:, cols]).reshape(8, 2, 2, 16, HALF).astype(BF16)
+            for c in range(2):
+                for part in range(2):
+                    wsum[half, c, part, pl.ds(cb * 8, 8)] = grad[:, c, part]
+            return carry
+
+        lax.fori_loop(0, 4, weight_grad, 0)
+
     peer = w + 1 - 2 * core
     sides = (n + 1 - 2 * lax.rem(n, 2), NARROW - 1 - n)
     parts = (lax.rem(n + 2, NARROW), sides[0], sides[1], n)
@@ -398,9 +410,9 @@
             device_id=to, device_id_type=MESH,
         )
 
-    def core_copy(half, j):
-        src = wsum.at[half, 1 - core, parts[j]]
-        return remote(src, core_got.at[half, parts[j]], (core_ss, core_rs), half * 4 + j, (peer, n))
+    def core_copy(half, part):
+        src = wsum.at[half, 1 - core, part]
+        return remote(src, core_got.at[half, part], (core_ss, core_rs), half * 4 + part, (peer, n))
 
     def chips(side):
         return pl.ds(16 * side, 16)
@@ -434,13 +446,14 @@
         units = pl.ds(0, 2) if piece == 0 else pl.ds(piece + 1, 1)
         return remote(cx_send.at[units, d - 1], cx_got.at[units, d - 1], (cx_ss, cx_rs), piece * 3 + d - 1, (w, to))
 
-    def core_start(half):
+    def core_start(half, first):
+        for part in (first, first + 1):
+            core_copy(half, part).start()
+
+    def core_step(half):
+        for part in range(4):
+            core_copy(half, part).wait_recv()
         for j in range(4):
-            core_copy(half, j).start()
-
-    def core_step(half):
-        for j in range(4):
-            core_copy(half, j).wait_recv()
             part = parts[j]
             core_sum[half, part] = (wsum[half, core, part].astype(F32) + core_got[half, part].astype(F32)).astype(BF16)
             if j == 0:
@@ -511,13 +524,17 @@
         cold_out[:, cols] = quarter(n)
 
     own0 = give(0)
-    sums(0)
-    core_start(0)
+    sums_a(0)
+    core_start(0, 2)
+    sums_b(0)
+    core_start(0, 0)
+    sums_a(1)
+    core_start(1, 2)
+    core_step(0)
+    sums_b(1)
+    core_start(1, 0)
     own1 = give(1)
     lax.fori_loop(1, WIDE, give_rest, 0)
-    core_step(0)
-    sums(1)
-    core_start(1)
     core_step(1)
     x_pass(0)
 
@@ -537,14 +554,14 @@
     own0.wait()
     own1.wait()
 
+    x_pass(1)
     x_step(0)
-    x_pass(1)
+    x_step(1)
     cold_step(0)
     y_step(0)
-    x_step(1)
-    z_step(0)
     cold_step(1)
     y_step(1)
+    z_step(0)
     cold_step(2)
     z_step(1)
     for half in range(2):
@@ -577,8 +594,8 @@
         for d in range(1, NARROW):
             cx_copy(piece, d).wait_send()
     for half in range(2):
-        for j in range(4):
-            core_copy(half, j).wait_send()
+        for part in range(4):
+            core_copy(half, part).wait_send()
         for side in range(2):
             x_copy(half, side, 0).wait_send()
             x_copy(half, side, 1).wait_send()
@@ -603,12 +620,13 @@
     item_owner, item_row, hot_row, hot_flag, seq_length, cold_table, hot_table, proj_weight, out_weight, norm_gain, cotangent
 ):
     vm = pl.BlockSpec(memory_space=pltpu.VMEM)
-    sm = pl.BlockSpec(memory_space=pltpu.SMEM)
     v = pltpu.VMEM
     dma = pltpu.SemaphoreType.DMA
     slots = WIDE * CAP
     block = (WIDE, 48, 256)
+    i32 = jnp.int32
     scratch = [
+        v((2, 1, LEN), i32), v((2, LEN), i32), v((2, LEN), i32), v((2, LEN), i32), pltpu.SMEM((2,), i32), v((1, D), F32),
         v((ROWS, D), BF16), v((TOK, D), BF16), v((D, 4 * D), BF16), v((D, D), BF16), v((TOK, D), BF16),
         v((32, 128), F32), v((8, 128), F32), v((WIDE, 1, 128), F32), v((WIDE, 1, 128), F32),
         v(block, BF16), v(block, BF16), v((slots, D), BF16), v((slots, TOK), BF16), v((TOK, TOK), BF16),
@@ -622,7 +640,7 @@
         v((2, 4, 8, 16, HALF), BF16), v((2, 3, 8, 16, HALF), BF16),
         v((2, 8, 16, HALF), BF16), v((2, 7, 16, HALF), BF16), v((2, 4, 16, HALF), F32),
         v((4, 3, 256, 128), BF16), v((4, 3, 256, 128), BF16), v((4, 256, slots), BF16), v((D, 8), F32),
-        dma((5,)), dma((2,)), dma((5,)), dma((8,)), dma((8,)), dma((3,)), dma((8,)), dma((8,)), dma((12,)), dma((12,)), dma((6,)), dma((6,)),
+        dma((11,)), dma((2,)), dma((5,)), dma((8,)), dma((8,)), dma((3,)), dma((8,)), dma((8,)), dma((12,)), dma((12,)), dma((6,)), dma((6,)),
         dma((14,)), dma((14,)), dma((6,)), dma((6,)), dma((9,)), dma((9,)),
     ]
     shape = jax.ShapeDtypeStruct
@@ -631,7 +649,7 @@
     parts = pl.pallas_call(
         kernel,
         out_shape=results,
-        in_specs=[vm] * 4 + [sm, vm] + [hbm] * 5,
+        in_specs=[hbm] * 11,
         out_specs=[vm] * 5,
         scratch_shapes=scratch,
         compiler_params=pltpu.CompilerParams(collective_id=0, has_side_effects=True, vmem_limit_bytes=62 * 1024 * 1024),

time: 129 us -> 124 us (0.961); the launches traced: 127 us -> 124 us
  Pallas kernels: 126 us -> 123 us
    pallas_call x1, Pallas kernels: 124 us -> 121 us  [local(): pl.pallas_call(kernel, out_shape=results, in_specs=[hbm] * 11, out_specs=...]
where the time goes in v4:
time: 124 us
  Pallas kernels  123 us (99%)
    pallas_call x1, Pallas kernels, local(): pl.pallas_call(kernel, out_shape=results, in_specs=[hbm] * 11, out_specs=...  121 us

profile of v4, /device:TPU:1, one launch (start us, length us, event | category | flops | bytes accessed | tf_op | source)
XLA Modules:
  0.0 123.8 jit_solution(8366253995136402341)
XLA Ops:
  0.6 121.1 %shard_map.146 = (f32[32,512]{1,0:T(8,128)}, f32[8,512]{1,0:T(8,128)}, f32[1,8]{1,0:T(1,128)}, f32[256,512]{1,0:T(8,128)}, f32[4,512]{1,0:T(4,128)}) custom-call(s32[2,1,512]{2,1,0:T(1,128)} %bitcast.5, s32[2,512]{1,0:T(2,128)} %row_in_in.1, s32[2,512]{1,0:T(2,128)} %hot_row_in.1, s32[2,512]{1,0:T(2,128)} %hot_flag_in.1, s32[2]{0:T(128)} %lens_in.1, ...), custom_call_target="tpu_custom_call" | custom-call | tf_op jit(solution)/shard_map/pallas_call | solution.py:649
  121.7 1.9 %shard_map.147 = (f32[32,512]{1,0:T(8,128)}, f32[8,512]{1,0:T(8,128)}, f32[1,8]{1,0:T(1,128)}, f32[256,512]{1,0:T(8,128)}, f32[4,512]{1,0:T(4,128)}) custom-call(f32[32,512]{1,0:T(8,128)} %get-tuple-element.15.refs_0_, f32[8,512]{1,0:T(8,128)} %get-tuple-element.16.refs_1_, f32[1,8]{1,0:T(1,128)} %get-tuple-element.17.refs_2_, ...), custom_call_target="tpu_custom_call" | custom-call | tf_op jit(solution)/shard_map/pallas_call | solution.py:660

commit v5 on v4

--- a/solution.py
+++ b/solution.py
@@ -535,8 +535,8 @@
     core_start(1, 0)
     own1 = give(1)
     lax.fori_loop(1, WIDE, give_rest, 0)
+    x_pass(0)
     core_step(1)
-    x_pass(0)
 
     asked = want[...].reshape(WIDE, 128)
     high = jnp.floor(asked * (1.0 / 32.0))
@@ -554,15 +554,15 @@
     own0.wait()
     own1.wait()
 
+    x_step(0)
     x_pass(1)
-    x_step(0)
+    cold_step(0)
     x_step(1)
-    cold_step(0)
     y_step(0)
     cold_step(1)
     y_step(1)
+    cold_step(2)
     z_step(0)
-    cold_step(2)
     z_step(1)
     for half in range(2):
         cols = slice(half * HALF, (half + 1) * HALF)

time: 124 us -> 124 us (level)
  no operation moved by 1% of the time
where the time goes in v5:
time: 124 us
  Pallas kernels  123 us (99%)
    pallas_call x1, Pallas kernels, local(): pl.pallas_call(kernel, out_shape=results, in_specs=[hbm] * 11, out_specs=...  121 us

profile of v5, /device:TPU:1, one launch (start us, length us, event | category | flops | bytes accessed | tf_op | source)
XLA Modules:
  0.0 123.8 jit_solution(9138991338783604725)
XLA Ops:
  0.6 121.0 %shard_map.146 = (f32[32,512]{1,0:T(8,128)}, f32[8,512]{1,0:T(8,128)}, f32[1,8]{1,0:T(1,128)}, f32[256,512]{1,0:T(8,128)}, f32[4,512]{1,0:T(4,128)}) custom-call(s32[2,1,512]{2,1,0:T(1,128)} %bitcast.5, s32[2,512]{1,0:T(2,128)} %row_in_in.1, s32[2,512]{1,0:T(2,128)} %hot_row_in.1, s32[2,512]{1,0:T(2,128)} %hot_flag_in.1, s32[2]{0:T(128)} %lens_in.1, ...), custom_call_target="tpu_custom_call" | custom-call | tf_op jit(solution)/shard_map/pallas_call | solution.py:649
  121.7 1.9 %shard_map.147 = (f32[32,512]{1,0:T(8,128)}, f32[8,512]{1,0:T(8,128)}, f32[1,8]{1,0:T(1,128)}, f32[256,512]{1,0:T(8,128)}, f32[4,512]{1,0:T(4,128)}) custom-call(f32[32,512]{1,0:T(8,128)} %get-tuple-element.15.refs_0_, f32[8,512]{1,0:T(8,128)} %get-tuple-element.16.refs_1_, f32[1,8]{1,0:T(1,128)} %get-tuple-element.17.refs_2_, ...), custom_call_target="tpu_custom_call" | custom-call | tf_op jit(solution)/shard_map/pallas_call | solution.py:660

commit v6 on v5

--- a/solution.py
+++ b/solution.py
@@ -59,7 +59,8 @@
 
 def kernel(
     owner_in, row_in_in, hot_row_in, hot_flag_in, lens_in, gain_in, table_in, hot_table_in, weight_in, out_weight_in, cot_in,
-    proj_out, out_out, gain_out, cold_out, hot_out,
+    proj_hbm, out_hbm, gain_hbm, cold_hbm, hot_hbm,
+    proj_out, out_out, gain_out, cold_out, hot_out, store_sem,
     owner, row_in, hot_row, hot_flag, lens, gain, table, hot_table, weight, out_weight, cot, tok, slots, req, want, reply, got, rows_in, place_t, hot_t, emb, normed, xhat, spread, acted, dact,
     attn, dattn, per_head, mixed, masked, mixed_cot, dhead, proj_cot, emb_grad, gain_sum,
     cold_send, cold_got, wsum, core_got, core_sum, x_got, x_on, x_on_got, x_sum, y_got, y_sum, z_got, gathered, cx_send, cx_got, quarter_t, turned,
@@ -559,11 +560,11 @@
     cold_step(0)
     x_step(1)
     y_step(0)
+    y_step(1)
     cold_step(1)
-    y_step(1)
-    cold_step(2)
     z_step(0)
     z_step(1)
+    cold_step(2)
     for half in range(2):
         cols = slice(half * HALF, (half + 1) * HALF)
         for d in range(1, NARROW):
@@ -578,14 +579,24 @@
                 hot_out[:, cols] = gathered[half, 3, 4 * k : 4 * k + 4]
 
     gain_out[...] = turned[pl.ds(pl.multiple_of(w * 8, 8), 8), :].T[0:1, :]
+    stores = [
+        pltpu.make_async_copy(src, dst, store_sem.at[i])
+        for i, (src, dst) in enumerate([(proj_out, proj_hbm), (out_out, out_hbm), (gain_out, gain_hbm), (hot_out, hot_hbm)])
+    ]
+    for store in stores:
+        store.start()
     for piece in range(3):
         for d in range(1, NARROW):
             cx_copy(piece, d).wait_recv()
-    for u in range(4):
-        total = cold_out[:, u * 128 : (u + 1) * 128]
-        for d in range(NARROW - 1):
-            total = total + cx_got[u, d].astype(F32)
-        cold_out[:, u * 128 : (u + 1) * 128] = total
+        units = (0, 1) if piece == 0 else (piece + 1,)
+        cols = slice(units[0] * 128, units[-1] * 128 + 128)
+        for u in units:
+            total = cold_out[:, u * 128 : (u + 1) * 128]
+            for d in range(NARROW - 1):
+                total = total + cx_got[u, d].astype(F32)
+            cold_out[:, u * 128 : (u + 1) * 128] = total
+        stores.append(pltpu.make_async_copy(cold_out.at[:, cols], cold_hbm.at[:, cols], store_sem.at[4 + piece]))
+        stores[-1].start()
 
     await_bytes(a2a_send.at[0], req.at[others])
     await_bytes(a2a_send.at[1], reply.at[others])
@@ -605,6 +616,8 @@
             g_copy(half, d).wait_send()
         for d in range(1, 8):
             z_copy(half, d).wait_send()
+    for store in stores:
+        store.wait()
 
 
 def finish(*refs):
@@ -626,6 +639,7 @@
     block = (WIDE, 48, 256)
     i32 = jnp.int32
     scratch = [
+        v((32, D), F32), v((8, D), F32), v((1, 8), F32), v((256, D), F32), v((4, D), F32), dma((7,)),
         v((2, 1, LEN), i32), v((2, LEN), i32), v((2, LEN), i32), v((2, LEN), i32), pltpu.SMEM((2,), i32), v((1, D), F32),
         v((ROWS, D), BF16), v((TOK, D), BF16), v((D, 4 * D), BF16), v((D, D), BF16), v((TOK, D), BF16),
         v((32, 128), F32), v((8, 128), F32), v((WIDE, 1, 128), F32), v((WIDE, 1, 128), F32),
@@ -650,7 +664,7 @@
         kernel,
         out_shape=results,
         in_specs=[hbm] * 11,
-        out_specs=[vm] * 5,
+        out_specs=[hbm] * 5,
         scratch_shapes=scratch,
         compiler_params=pltpu.CompilerParams(collective_id=0, has_side_effects=True, vmem_limit_bytes=62 * 1024 * 1024),
     )(

time: 124 us -> 124 us (level)
  no operation moved by 1% of the time
where the time goes in v6:
time: 124 us
  Pallas kernels  123 us (99%)
    pallas_call x1, Pallas kernels, local(): pl.pallas_call(kernel, out_shape=results, in_specs=[hbm] * 11, out_specs=...  121 us

profile of v6, /device:TPU:1, one launch (start us, length us, event | category | flops | bytes accessed | tf_op | source)
XLA Modules:
  0.0 123.9 jit_solution(3843684504716166241)
XLA Ops:
  0.6 121.2 %shard_map.146 = (f32[32,512]{1,0:T(8,128)}, f32[8,512]{1,0:T(8,128)}, f32[1,8]{1,0:T(1,128)}, f32[256,512]{1,0:T(8,128)}, f32[4,512]{1,0:T(4,128)}) custom-call(s32[2,1,512]{2,1,0:T(1,128)} %bitcast.5, s32[2,512]{1,0:T(2,128)} %row_in_in.1, s32[2,512]{1,0:T(2,128)} %hot_row_in.1, s32[2,512]{1,0:T(2,128)} %hot_flag_in.1, s32[2]{0:T(128)} %lens_in.1, ...), custom_call_target="tpu_custom_call" | custom-call | tf_op jit(solution)/shard_map/pallas_call | solution.py:663
  121.8 1.9 %shard_map.147 = (f32[32,512]{1,0:T(8,128)}, f32[8,512]{1,0:T(8,128)}, f32[1,8]{1,0:T(1,128)}, f32[256,512]{1,0:T(8,128)}, f32[4,512]{1,0:T(4,128)}) custom-call(f32[32,512]{1,0:T(8,128)} %get-tuple-element.15.refs_0_, f32[8,512]{1,0:T(8,128)} %get-tuple-element.16.refs_1_, f32[1,8]{1,0:T(1,128)} %get-tuple-element.17.refs_2_, ...), custom_call_target="tpu_custom_call" | custom-call | tf_op jit(solution)/shard_map/pallas_call | solution.py:674

commit v7 on v6

--- a/solution.py
+++ b/solution.py
@@ -107,8 +107,7 @@
     upper = onehot(iota((128, 128), 0) < iota((128, 128), 1))
     sub = iota((128, 128), 0)
     carry = jnp.zeros((128, 1), F32)
-    req_hi = jnp.zeros((128, 128), F32)
-    req_lo = jnp.zeros((128, 128), F32)
+    req_both = jnp.zeros((128, 256), F32)
     for a in range(8):
         own = tok[a : a + 1, :]
         row = tok[8 + a : 9 + a, :]
@@ -122,9 +121,9 @@
         high = jnp.floor(row * (1.0 / 32.0))
         low = row - 32.0 * high
         ranked = sub == rank
-        req_hi = req_hi + mm_nt(owns_b, jnp.where(ranked, high, 0.0).astype(BF16))
-        req_lo = req_lo + mm_nt(owns_b, jnp.where(ranked, low, 0.0).astype(BF16))
-    asked = 32.0 * req_hi + req_lo
+        both = jnp.concatenate([jnp.where(ranked, high, 0.0), jnp.where(ranked, low, 0.0)], axis=0)
+        req_both = req_both + mm_nt(owns_b, both.astype(BF16))
+    asked = 32.0 * req_both[:, :128] + req_both[:, 128:]
     for o in range(WIDE):
         req[o] = asked[o : o + 1, :]
 
@@ -563,8 +562,8 @@
     y_step(1)
     cold_step(1)
     z_step(0)
+    cold_step(2)
     z_step(1)
-    cold_step(2)
     for half in range(2):
         cols = slice(half * HALF, (half + 1) * HALF)
         for d in range(1, NARROW):

time: 124 us -> 123 us (level)
  Pallas kernels: 123 us -> 121 us
    pallas_call x1, Pallas kernels: 121 us -> 119 us  [local(): pl.pallas_call(kernel, out_shape=results, in_specs=[hbm] * 11, out_specs=...]
where the time goes in v7:
time: 123 us; the launch traced here: 122 us
  Pallas kernels  121 us (98%)
    pallas_call x1, Pallas kernels, local(): pl.pallas_call(kernel, out_shape=results, in_specs=[hbm] * 11, out_specs=...  119 us

profile of v7, /device:TPU:1, one launch (start us, length us, event | category | flops | bytes accessed | tf_op | source)
XLA Modules:
  0.0 122.1 jit_solution(1691389867802840)
XLA Ops:
  0.6 119.4 %shard_map.146 = (f32[32,512]{1,0:T(8,128)}, f32[8,512]{1,0:T(8,128)}, f32[1,8]{1,0:T(1,128)}, f32[256,512]{1,0:T(8,128)}, f32[4,512]{1,0:T(4,128)}) custom-call(s32[2,1,512]{2,1,0:T(1,128)} %bitcast.5, s32[2,512]{1,0:T(2,128)} %row_in_in.1, s32[2,512]{1,0:T(2,128)} %hot_row_in.1, s32[2,512]{1,0:T(2,128)} %hot_flag_in.1, s32[2]{0:T(128)} %lens_in.1, ...), custom_call_target="tpu_custom_call" | custom-call | tf_op jit(solution)/shard_map/pallas_call | solution.py:662
  120.0 1.9 %shard_map.147 = (f32[32,512]{1,0:T(8,128)}, f32[8,512]{1,0:T(8,128)}, f32[1,8]{1,0:T(1,128)}, f32[256,512]{1,0:T(8,128)}, f32[4,512]{1,0:T(4,128)}) custom-call(f32[32,512]{1,0:T(8,128)} %get-tuple-element.15.refs_0_, f32[8,512]{1,0:T(8,128)} %get-tuple-element.16.refs_1_, f32[1,8]{1,0:T(1,128)} %get-tuple-element.17.refs_2_, ...), custom_call_target="tpu_custom_call" | custom-call | tf_op jit(solution)/shard_map/pallas_call | solution.py:673
